TPU v7x, 256 devices: a whole 4x4x8 slice. The times are simulated.
256 devices in a mesh: group: 4 (over y_lo, core), blk: 64 (over z, x, y_hi).
Axes of the slice: x: 4, y: 4 (y_hi: 2, y_lo: 2; y = y_hi * 2 + y_lo), z: 8, core: 2. Of those that a mesh axis runs over, the one named last changes fastest.
Arguments:
- features: bfloat16 [8192, 2048], P('blk', 'group'), may hold values from -16 to 16
- weight: bfloat16 [2048, 256], P('group'), may hold values from -0.125 to 0.125
- queue: bfloat16 [131072, 256], P(('group', 'blk')), may hold values from -0.5 to 0.5, as said below
- fresh_keys: bfloat16 [8192, 256], P('blk'), may hold values from -0.3984375 to 0.3984375
- positives: int32 [8192], P('blk'), may hold values from 0 to 8191, each once
- write_slot: int32 [1], replicated, may hold values from 0 to 122880
Outputs:
- query_loss: float32 [8192], P('blk')
- weight_grad: float32 [2048, 256], P(('group', 'blk'))
- new_queue: bfloat16 [131072, 256], P(('group', 'blk'))
Inputs may be any that keep to these rules, and one draw needn't show every extreme that they name: `queue`: scaled item keys.
All inputs are finite; a program needn't handle non-finite values.
Results may differ from a plain program's by a relative error of at most 0.003.
The roundings to bfloat16 on the way count: a program that leaves them out, or rounds other values in their place, can miss the bound.
Values may be sent and summed in bfloat16 or wider, within the bound.
A program may use at most 64 MiB of HBM per device.

v0:
```python
import math

import jax
import jax.numpy as jnp
from jax import lax
from jax.sharding import PartitionSpec as P

epsilon = 1e-06
inverse_sharpness_factor = 8.0


def from_everyone(array, axis):
    copies = jnp.broadcast_to(array, (lax.axis_size(axis), *array.shape))
    return lax.all_to_all(copies, axis, split_axis=0, concat_axis=0, tiled=True)


def taken_together(array, axis):
    everything = from_everyone(array, axis)
    return jnp.sum(everything, axis=0)


def in_one_piece(arrays, axis, dim, along):
    both = jnp.concatenate(arrays, axis=along)
    whole, at, finished = (lax.all_gather(both, axis, axis=dim, tiled=True), 0, [])
    for a in arrays:
        finished.append(lax.slice_in_dim(whole, at, at + a.shape[along], axis=along))
        at += a.shape[along]
    return tuple(finished)


def in_one_piece_2(arrays, axis, dim, along):
    widths = [math.prod(a.shape[along:]) for a in arrays]
    both = jnp.concatenate(
        [a.reshape(*a.shape[:along], w) for a, w in zip(arrays, widths)], axis=along
    )
    whole = lax.psum_scatter(both, axis, scatter_dimension=dim, tiled=True)
    parts = jnp.split(whole, [sum(widths[:k]) for k in range(1, len(widths))], axis=along)
    return tuple((b.reshape(*whole.shape[:along], *a.shape[along:]) for a, b in zip(arrays, parts)))


def together(arrays, axis):
    vector, at, finished = (jnp.concatenate([a.reshape(-1) for a in arrays]), 0, [])
    total = taken_together(vector, axis)
    for a in arrays:
        finished.append(total[at : at + a.size].reshape(a.shape))
        at += a.size
    return tuple(finished)


def split_up(array, dim, length):
    before, after = (array.shape[:dim], array.shape[dim + 1 :])
    return jnp.moveaxis(array.reshape(*before, length, -1, *after), dim, 0)


def sum_at_owner(array, axis, dim):
    length = lax.axis_size(axis)
    parts = lax.all_to_all(split_up(array, dim, length), axis, 0, 0, tiled=True)
    return jnp.sum(parts, axis=0)


def local(features, weight, queue, fresh_keys, positives, write_slot):
    partial_proj = jnp.dot(features, weight, preferred_element_type=jnp.float32)
    projected = taken_together(partial_proj, "group")
    length = jnp.sqrt(jnp.sum(projected * projected, axis=1, keepdims=True) + epsilon)
    unit_rows = projected / length
    query_rows = unit_rows.astype(jnp.bfloat16)
    all_queries, all_fresh = in_one_piece((query_rows, fresh_keys), "blk", 0, 1)
    query_total = all_queries.shape[0]
    key_width = all_queries.shape[1]
    blk_count = lax.axis_size("blk")
    block_rows = 512
    query_blocks = all_queries.reshape(query_total // block_rows, block_rows, key_width)

    def score_block(carry, rows_now):
        similarity_matrix = jnp.einsum(
            "qc,sc->qs", rows_now, queue, preferred_element_type=jnp.float32
        )
        exponentials = jnp.exp(inverse_sharpness_factor * similarity_matrix)
        denominator = jnp.sum(exponentials, axis=1)
        numerator = jnp.dot(
            exponentials.astype(jnp.bfloat16), queue, preferred_element_type=jnp.float32
        )
        return (carry, (numerator, denominator))

    _, (numer_blocks, denom_blocks) = lax.scan(score_block, jnp.float32(0.0), query_blocks)
    numer_all = numer_blocks.reshape(query_total, key_width)
    denom_all = denom_blocks.reshape(query_total)
    numer_part, denom_part = in_one_piece_2((numer_all, denom_all), "blk", 0, 1)
    numerator, denominator = together((numer_part, denom_part), "group")
    paired_encodings = jnp.take(all_fresh, positives, axis=0).astype(jnp.float32)
    pair_score = inverse_sharpness_factor * jnp.sum(
        query_rows.astype(jnp.float32) * paired_encodings, axis=1
    )
    pair_weight = jnp.exp(pair_score)
    probability_mass = pair_weight + denominator
    query_loss = jnp.log(probability_mass) - pair_score
    query_derivative = inverse_sharpness_factor * (
        (pair_weight[:, None] * paired_encodings + numerator) / probability_mass[:, None]
        - paired_encodings
    )
    along = jnp.sum(query_derivative * unit_rows, axis=1, keepdims=True)
    grad_projected = ((query_derivative - along * unit_rows) / length).astype(jnp.bfloat16)
    weight_grad = sum_at_owner(
        lax.dot_general(
            features, grad_projected, (((0,), (0,)), ((), ())), preferred_element_type=jnp.float32
        ),
        "blk",
        0,
    )
    slot_count = queue.shape[0]
    device_index = lax.axis_index("group") * blk_count + lax.axis_index("blk")
    window_start = write_slot[0]
    slot_index = device_index * slot_count + jnp.arange(slot_count, dtype=jnp.int32)
    offset = slot_index - window_start
    in_window = (offset >= 0) & (offset < query_total)
    picked = jnp.take(all_fresh, jnp.clip(offset, 0, query_total - 1), axis=0)
    new_queue = jnp.where(in_window[:, None], picked, queue)
    return (query_loss, weight_grad, new_queue)


def solution(mesh):
    in_specs = (
        P("blk", "group"),
        P("group", None),
        P(("group", "blk"), None),
        P("blk", None),
        P("blk"),
        P(),
    )
    out_specs = (P("blk"), P(("group", "blk"), None), P(("group", "blk"), None))
    return jax.shard_map(local, mesh=mesh, in_specs=in_specs, out_specs=out_specs, check_vma=False)
```

profile of v0, /device:TPU:1, one launch (start us, length us, event | category | flops | bytes accessed | tf_op | source)
XLA Modules:
  0.0 663.6 jit_solution(13133228975736221165)
XLA Ops:
  9.3 13.4 %all_to_all.16 = f32[4,128,256]{2,1,0:T(8,128)S(1)} all-to-all(f32[4,128,256]{2,1,0:T(8,128)S(1)} %broadcast_in_dim.55), channel_id=1, replica_groups=mesh['group'=4,'blk'=64] {'group'}, dimensions={0} | all-to-all | bytes 1048576 | tf_op jit(solution)/shard_map/all_to_all | solution.py:14
  23.0 1.5 pad_maximum_fusion.2
  24.6 146.5 %all-gather.2.cloned.1.call-done = bf16[8192,512]{1,0:T(8,128)(2,1)} async-done(((bf16[128,512]{1,0:T(8,128)(2,1)}), bf16[8192,512]{1,0:T(8,128)(2,1)}) %all-gather.2.cloned.1.call-update) | async-done | bytes 8388624 | tf_op jit(solution)/shard_map/all_gather | solution.py:24
  171.1 5.8 fusion.18
  176.8 40.7 %while.12 = (s32[]{:T(128)}, f32[16,512,256]{2,1,0:T(8,128)}, f32[16,512]{1,0:T(8,128)S(1)}, bf16[16,512,256]{2,1,0:T(8,128)(2,1)}, bf16[512,256]{1,0:T(8,128)(2,1)S(1)}, /*index=5*/s32[]{:T(128)}, s32[]{:T(128)}) while((s32[]{:T(128)}, f32[16,512,256]{2,1,0:T(8,128)}, f32[16,512]{1,0:T(8,128)S(1)}, bf16[16,512,256]{2,1,0:T(8,128)(2,1)}, ...), condition=%wide.region_5.6_spmd, body=%wide.region_3.5_spmd.sunk | while | flops 269221376 | bytes 2365537 | solution.py:85
  176.8 1.3 fusion.34
  179.4 1.3 fusion.34
  181.9 1.3 fusion.34
  184.5 1.3 fusion.34
  187.0 1.3 fusion.34
  189.5 1.3 fusion.34
  192.1 1.3 fusion.34
  194.6 1.3 fusion.34
  197.2 1.3 fusion.34
  198.5 1.2 fusion.35
  199.7 1.3 fusion.34
  201.1 1.2 fusion.35
  202.3 1.3 fusion.34
  204.9 1.3 fusion.34
  207.4 1.3 fusion.34
  210.0 1.3 fusion.34
  212.5 1.3 fusion.34
  215.0 1.3 fusion.34
  217.6 8.9 %copy.16 = f32[8192,256]{0,1:T(8,128)} copy(f32[8192,256]{1,0:T(8,128)} %bitcast.45) | data formatting | bytes 16777216 | tf_op jit(solution)/shard_map/reshape | solution.py:86
  226.5 7.7 %pad_maximum_fusion = f32[8192,257]{0,1:T(8,128)} fusion(f32[8192,1]{0,1:T(1,128)S(1)} %bitcast.49, f32[8192,256]{0,1:T(8,128)} %copy.16), kind=kLoop, calls=%fused_computation.10 | loop fusion | flops 2105344 | bytes 16842752 | tf_op jit(solution)/shard_map/concatenate | solution.py:33
  234.9 334.1 %reduce-scatter.2.cloned.1.call-done = f32[128,257]{0,1:T(8,128)} async-done(((f32[8192,257]{0,1:T(8,128)}), f32[128,257]{0,1:T(8,128)}) %reduce-scatter.2.cloned.1.call-update) | async-done | bytes 131600 | tf_op jit(solution)/shard_map/reduce_scatter | solution.py:36
  571.9 51.7 %all-to-all-start.1 = ((f32[4,1,32896]{2,1,0:T(1,128)}), f32[4,1,32896]{2,1,0:T(1,128)S(1)}, u32[]{:S(2)}, u32[]{:S(2)}) async-start(f32[4,1,32896]{2,1,0:T(1,128)} %broadcast_in_dim.61), calls=%async_computation.2 | async-start | bytes 1052672 | tf_op jit(solution)/shard_map/all_to_all | solution.py:14
  623.6 3.5 gather_fusion
  627.3 4.3 all-to-all-done.1
  634.3 5.2 all-to-all-start.2
  640.2 4.3 gather_fusion.1
  645.4 10.7 %all-to-all-done.2 = f32[64,8,256]{2,1,0:T(8,128)S(1)} async-done(((f32[64,8,256]{2,1,0:T(8,128)}), f32[64,8,256]{2,1,0:T(8,128)S(1)}, u32[]{:S(2)}, u32[]{:S(2)}) %all-to-all-start.2) | async-done | bytes 524320 | tf_op jit(solution)/shard_map/all_to_all | solution.py:57
  (73 shorter events, 27.5 us)
Async XLA Ops:
  7.2 1.0 copy-start
  7.2 163.9 %all-gather.2.cloned.1.call-start = ((), (), s32[]{:S(2)}) async-start(), calls=%async_computation.4 | async-start | bytes 8519680 | tf_op jit(solution)/shard_map/all_gather | solution.py:24
  24.5 544.5 %reduce-scatter.2.cloned.1.call-start = ((), (), s32[]{:S(2)}) async-start(), calls=%async_computation.5 | async-start | bytes 8785920 | tf_op jit(solution)/shard_map/reduce_scatter | solution.py:36
  24.6 152.3 %copy-start.1 = (bf16[512,256]{1,0:T(8,128)(2,1)S(1)}, bf16[512,256]{1,0:T(8,128)(2,1)}, u32[]{:S(2)}) copy-start(bf16[512,256]{1,0:T(8,128)(2,1)} %param.10) | copy-start | bytes 786436
  234.3 0.7 copy-start.3
  234.3 398.6 %copy-start.2 = (bf16[128,512]{1,0:T(8,128)(2,1)S(1)}, bf16[128,512]{1,0:T(8,128)(2,1)}, u32[]{:S(2)}) copy-start(bf16[128,512]{1,0:T(8,128)(2,1)} %param.8) | copy-start | bytes 393220
  571.9 59.7 %all-to-all-start.1 = ((f32[4,1,32896]{2,1,0:T(1,128)}), f32[4,1,32896]{2,1,0:T(1,128)S(1)}, u32[]{:S(2)}, u32[]{:S(2)}) async-start(f32[4,1,32896]{2,1,0:T(1,128)} %broadcast_in_dim.61), calls=%async_computation.2 | async-start | bytes 1052672 | tf_op jit(solution)/shard_map/all_to_all | solution.py:14
  634.3 21.8 %all-to-all-start.2 = ((f32[64,8,256]{2,1,0:T(8,128)}), f32[64,8,256]{2,1,0:T(8,128)S(1)}, u32[]{:S(2)}, u32[]{:S(2)}) async-start(f32[64,8,256]{2,1,0:T(8,128)} %bitcast.7), calls=%async_computation.3 | async-start | bytes 1048576 | tf_op jit(solution)/shard_map/all_to_all | solution.py:57
Sparse Core Ops, SparseCore 0:
  24.6 146.3 all-gather.1
  234.4 334.5 reduce-scatter.1
where the time goes:
time: 666 us; the launch traced here: 664 us
  waiting for transfers between devices  496 us (74%)
  starting transfers between devices  57 us (9%)
  matrix products  41 us (6%)
  local copies, waits for them, and re-layouts  28.9 us (4%)
  between operations  14.9 us (2%)
  blocking collectives  13.4 us (2%)
  other arithmetic  12.5 us (2%)
    reduce_scatter x1, waiting for transfers between devices, in_one_piece_2(): whole = lax.psum_scatter(both, axis, scatter_dimension=dim, tiled=True)  334 us
    all_gather x1, waiting for transfers between devices, in_one_piece(): lax.all_gather(both, axis, axis=dim, tiled=True)  146 us
    all_to_all x1, starting transfers between devices, from_everyone(): return lax.all_to_all(copies, axis, split_axis=0, concat_axis=0, tiled=True)  51.7 us
    dot_general x16, matrix products, score_block(): jnp.einsum('qc,sc->qs', rows_now, queue, preferred_element_type=jnp.float32)  21 us
    dot_general x16, matrix products, score_block(): jnp.dot(exponentials.astype(jnp.bfloat16), queue, preferred_element_type=...  18.5 us
    all_to_all x1, blocking collectives, from_everyone(): return lax.all_to_all(copies, axis, split_axis=0, concat_axis=0, tiled=True)  13.4 us
  transfers between devices with their start and end apart: 4, of which 4 were waited for; matrix products, arithmetic and copies ran while one was open for 1% of the time, Pallas kernels for 0%

commit v1 on v0

v1 whole, which is shorter than its diff:
```python
import functools
import math

import jax
import jax.numpy as jnp
from jax import lax
from jax.experimental import pallas as pl
from jax.experimental.pallas import tpu as pltpu
from jax.sharding import PartitionSpec as P

EPSILON = 1e-06
SHARP = 8.0
SHARP_LOG2E = SHARP * math.log2(math.e)

Z, X, Y, CORES = 8, 4, 4, 2
ROWS = 32
WIDTH = 256
SLOT_ROWS = 512
QUERIES = 8192
F32 = jnp.float32
BF16 = jnp.bfloat16
COPIES = 128


def lane_sums(e):
    d = e[:, 0:128]
    for i in range(1, e.shape[1] // 128):
        d = d + e[:, 128 * i : 128 * (i + 1)]
    return d


def kernel(
    features,
    weight,
    queue,
    fresh,
    positives,
    write_slot,
    loss_out,
    wgrad_out,
    queue_out,
    proj,
    proj_in,
    queries,
    keys,
    fresh_all,
    pos_all,
    pick_out,
    pick_in,
    feat_t,
    num_out,
    num_in,
    numz_out,
    numz_in,
    den_out,
    den_in,
    denz_out,
    denz_in,
    gp_all,
    loss_rows,
    loss_in,
    wg,
    wg_in,
    wgz_out,
    wgz_in,
    wgy_out,
    wgy_in,
    send_sem,
    recv_sem,
):
    g = lax.axis_index("group")
    b = lax.axis_index("blk")
    y_lo, c = g // 2, g % 2
    z, x, y_hi = b // 8, (b // 2) % 4, b % 2
    y = 2 * y_hi + y_lo
    me_col = y * 2 + c

    def device(zz, xx, yy, cc):
        return {"group": (yy % 2) * 2 + cc, "blk": zz * 8 + xx * 2 + yy // 2}

    started = []

    def send(src, dst, to):
        at = len(started)
        copy = pltpu.make_async_remote_copy(
            src_ref=src,
            dst_ref=dst,
            send_sem=send_sem.at[at],
            recv_sem=recv_sem.at[at],
            device_id=to,
            device_id_type=pl.DeviceIdType.MESH,
        )
        copy.start()
        started.append(copy)
        return copy

    column = [(dy, dc) for dy in (0, 1, 3, 2) for dc in (1, 0) if (dy, dc) != (0, 0)]
    z_order = (1, 7, 2, 6, 3, 5, 4)
    x_order = (1, 3, 2)

    barrier = pltpu.get_barrier_semaphore()
    peers = [device(z, x, (y + dy) % 4, (c + dc) % 2) for dy, dc in column]
    peers += [device((z + d) % 8, x, y, c) for d in z_order]
    peers += [device(z, (x + d) % 4, y, c) for d in x_order]
    for p in peers:
        pl.semaphore_signal(barrier, inc=1, device_id=p, device_id_type=pl.DeviceIdType.MESH)

    proj[...] = jnp.dot(features[...], weight[...], preferred_element_type=F32).reshape(
        4, ROWS, WIDTH
    )
    fresh_all[z, x] = fresh[pl.ds(pl.multiple_of(g * ROWS, ROWS), ROWS), :]
    pos_all[0] = jnp.broadcast_to(positives[...], (8, 128))
    keys[me_col] = queue[...]
    pl.semaphore_wait(barrier, len(peers))

    group_peers = []
    for s in (1, 2, 3):
        yy, cc = 2 * y_hi + (y_lo + s // 2) % 2, (c + s % 2) % 2
        group_peers.append((s, yy, cc))
    proj_copies = [
        send(proj.at[(yy % 2) * 2 + cc], proj_in.at[s - 1], device(z, x, yy, cc))
        for s, yy, cc in group_peers
    ]

    up, down = (y + 1) % 4, (y + 3) % 4
    far = (y + 2) % 4
    other = 1 - c
    to_up, to_down = device(z, x, up, c), device(z, x, down, c)
    to_other = device(z, x, y, other)
    mine = keys.at[me_col]
    key_up = send(queue, mine, to_up)
    key_down = send(queue, mine, to_down)
    key_other = send(queue, mine, to_other)
    pos_copy = send(pos_all.at[0], pos_all.at[1], device(z, x, far, c))

    for copy in proj_copies:
        copy.wait_recv()
    projected = proj[g] + proj_in[0] + proj_in[1] + proj_in[2]
    length = jnp.sqrt(jnp.sum(projected * projected, axis=1, keepdims=True) + EPSILON)
    unit = projected / length
    query = unit.astype(BF16)
    queries[x, z] = query
    own_q = queries.at[x, z]
    qz = {d: send(own_q, own_q, device((z + d) % 8, x, y, c)) for d in z_order}
    qx = {(d, 0): send(own_q, own_q, device(z, (x + d) % 4, y, c)) for d in x_order}
    own_f = fresh_all.at[z, x]
    fz = [send(own_f, own_f, device((z + d) % 8, x, y, c)) for d in z_order]
    feat_t[...] = features[...].T
    for d in z_order:
        qz[d].wait_recv()
        block = queries.at[x, (z + 8 - d) % 8]
        for e in x_order:
            qx[e, d] = send(block, block, device(z, (x + e) % 4, y, c))

    key_up.wait_recv()
    from_down = keys.at[down * 2 + c]
    half = SLOT_ROWS // 2
    low, high = pl.ds(0, half), pl.ds(half, half)
    far_low = send(from_down.at[low], from_down.at[low], to_up)
    down_other = send(from_down, from_down, to_other)
    key_down.wait_recv()
    from_up = keys.at[up * 2 + c]
    far_high = send(from_up.at[high], from_up.at[high], to_down)
    up_other = send(from_up, from_up, to_other)
    from_far = keys.at[far * 2 + c]
    far_low.wait_recv()
    far_low_other = send(from_far.at[low], from_far.at[low], to_other)
    far_high.wait_recv()
    far_high_other = send(from_far.at[high], from_far.at[high], to_other)
    for copy in (key_other, down_other, up_other, far_low_other, far_high_other):
        copy.wait_recv()

    diagonal = lax.broadcasted_iota(jnp.int32, (ROWS, 128), 0) == lax.broadcasted_iota(
        jnp.int32, (ROWS, 128), 1
    )

    def tile(xx):
        q = queries[xx].reshape(Z * ROWS, WIDTH)
        num = den = None
        for j in range(8):
            k = keys[j]
            s = lax.dot_general(q, k, (((1,), (1,)), ((), ())), preferred_element_type=F32)
            e = jnp.exp2(s * SHARP_LOG2E)
            part = jnp.dot(e.astype(BF16), k, preferred_element_type=F32)
            sums = lane_sums(e)
            num = part if num is None else num + part
            den = sums if den is None else den + sums
        column_sums = jnp.sum(den, axis=1, keepdims=True).reshape(Z, ROWS, 1)
        den_rows = jnp.sum(jnp.where(diagonal[None], column_sums, 0.0), axis=1)
        return num.reshape(Z, ROWS, WIDTH), den_rows

    num_copies, den_copies = [], []

    def foreign_tile(i):
        d = x_order[i]
        for dz in (0, *z_order):
            qx[d, dz].wait_recv()
        owner = (x + 4 - d) % 4
        num, den = tile(owner)
        num_out[i] = num.astype(BF16)
        den_out[i] = den
        to = device(z, owner, y, c)
        den_copies.append(send(den_out.at[i], den_in.at[i], to))
        num_copies.append(send(num_out.at[i], num_in.at[i], to))

    foreign_tile(0)
    for copy in fz:
        copy.wait_recv()
    fresh_line = fresh_all.at[:, x]
    fx = [send(fresh_line, fresh_line, device(z, (x + d) % 4, y, c)) for d in x_order]
    foreign_tile(1)
    foreign_tile(2)

    for copy in fx:
        copy.wait_recv()
    pos_copy.wait_recv()
    lanes = lax.broadcasted_iota(jnp.int32, (128, 128), 1)
    offset = me_col * ROWS
    held = fresh_all[...].reshape(Z * X * ROWS, WIDTH)
    for r in range(2):
        wanted = jnp.broadcast_to(pos_all[r, 0:1, :], (128, 128)).astype(F32).T
        hits = []
        for m in range(8):
            at = 128 * m + lanes
            key = (at // ROWS) * WIDTH + offset + at % ROWS
            hits.append(jnp.where(wanted == key.astype(F32), 1.0, 0.0).astype(BF16))
        found = jnp.dot(jnp.concatenate(hits, axis=1), held, preferred_element_type=F32)
        found = found.astype(BF16).reshape(4, ROWS, WIDTH)
        for gg in range(4):
            pick_out[((y_hi + r) % 2) * 4 + gg, 0] = found[gg]

    slot = write_slot[0]

    def window(gg, bb):
        first = (gg * 64 + bb) * SLOT_ROWS - slot
        cycle = lax.shift_right_arithmetic(first, 8)
        return first, jnp.clip(cycle, 0, QUERIES // 256 - 3)

    for target in range(8):
        _, cycle = window(target % 4, z * 8 + x * 2 + target // 4)
        for k in range(3):
            at = cycle + k
            pick_out[target, 1 + k] = fresh_all[lax.shift_right_arithmetic(at, 2), at & 3]
    picks = []
    for dy, dc in column:
        yy, cc = (y + dy) % 4, (c + dc) % 2
        picks.append(send(pick_out.at[yy * 2 + cc], pick_in.at[me_col], device(z, x, yy, cc)))
    pick_in[me_col] = pick_out[me_col]

    num, den = tile(x)
    for i in range(3):
        den_copies[i].wait_recv()
        den = den + den_in[i]
        num_copies[i].wait_recv()
        num = num + num_in[i].astype(F32)
    numz_out[...] = num.astype(BF16)
    denz_out[...] = jnp.broadcast_to(den[:, None, :], (Z, 8, 128))
    numz, denz = [], []
    for i, d in enumerate(z_order):
        zz = (z + d) % 8
        to = device(zz, x, y, c)
        denz.append(send(denz_out.at[zz], denz_in.at[i], to))
        numz.append(send(numz_out.at[zz], numz_in.at[i], to))

    for copy in picks:
        copy.wait_recv()
    first, cycle = window(g, b)
    arrived = pick_in[...].reshape(1024, WIDTH)
    j = lax.broadcasted_iota(jnp.int32, (1, 1024), 1)
    kind = (j // ROWS) % 4
    held_key = (cycle + kind - 1) * 256 + (j // 128) * ROWS + j % ROWS
    held_key = jnp.where(kind == 0, -SLOT_ROWS * 1024, held_key)
    t = first + lax.broadcasted_iota(jnp.int32, (SLOT_ROWS, 1), 0)
    for r in range(0, SLOT_ROWS, 128):
        rows = t[r : r + 128]
        hit = jnp.where(rows == held_key, 1.0, 0.0).astype(BF16)
        moved = jnp.dot(hit, arrived, preferred_element_type=F32)
        old = queue[r : r + 128, :].astype(F32)
        inside = (rows >= 0) & (rows < QUERIES)
        queue_out[r : r + 128, :] = jnp.where(inside, moved, old).astype(BF16)
    positive = pick_in[0, 0].astype(F32)
    for src in range(1, 8):
        positive = positive + pick_in[src, 0].astype(F32)
    score = SHARP * jnp.sum(query.astype(F32) * positive, axis=1, keepdims=True)
    weight_p = jnp.exp(score)

    numerator = numz_out[z].astype(F32)
    den_row = denz_out[z]
    for i in range(7):
        denz[i].wait_recv()
        den_row = den_row + denz_in[i]
        numz[i].wait_recv()
        numerator = numerator + numz_in[i].astype(F32)
    denominator = jnp.sum(
        jnp.where(diagonal, jnp.broadcast_to(den_row[0:1, :], (ROWS, 128)), 0.0),
        axis=1,
        keepdims=True,
    )
    mass = weight_p + denominator
    loss = jnp.log(mass) - score
    grad = SHARP * ((weight_p * positive + numerator) / mass - positive)
    along = jnp.sum(grad * unit, axis=1, keepdims=True)
    grad_projected = ((grad - along * unit) / length).astype(BF16)
    gp_all[g] = grad_projected
    place = lax.broadcasted_iota(jnp.int32, (ROWS, 128), 0) + g * ROWS == (
        lax.broadcasted_iota(jnp.int32, (ROWS, 128), 1)
    )
    loss_row = jnp.sum(jnp.where(place, loss, 0.0), axis=0, keepdims=True)
    loss_rows[...] = jnp.broadcast_to(loss_row, (8, 128))
    gps = [send(gp_all.at[g], gp_all.at[g], device(z, x, yy, cc)) for _, yy, cc in group_peers]
    losses = [
        send(loss_rows, loss_in.at[s - 1], device(z, x, yy, cc)) for s, yy, cc in group_peers
    ]
    for copy in gps:
        copy.wait_recv()
    wg[...] = jnp.dot(
        feat_t[...], gp_all[...].reshape(128, WIDTH), preferred_element_type=F32
    ).reshape(Z, X, 16, WIDTH)
    wgx = []
    for i, d in enumerate(x_order):
        xx = (x + d) % 4
        wgx.append(send(wg.at[:, xx], wg_in.at[i], device(z, xx, y, c)))
    for i, copy in enumerate(losses):
        copy.wait_recv()
    loss_out[...] = (loss_rows[...] + loss_in[0] + loss_in[1] + loss_in[2])[0:1, :]
    for copy in wgx:
        copy.wait_recv()
    wgz_out[...] = wg[:, x] + wg_in[0] + wg_in[1] + wg_in[2]
    wgz = []
    for i, d in enumerate(z_order):
        zz = (z + d) % 8
        wgz.append(send(wgz_out.at[zz], wgz_in.at[i], device(zz, x, y, c)))
    total = wgz_out[z]
    for i in range(7):
        wgz[i].wait_recv()
        total = total + wgz_in[i]
    wgy_out[...] = total.reshape(2, 8, WIDTH)
    wgy = send(wgy_out.at[1 - y_hi], wgy_in, device(z, x, far, c))
    wgy.wait_recv()
    wgrad_out[...] = wgy_out[y_hi] + wgy_in[...]

    for copy in started:
        copy.wait_send()


def local(features, weight, queue, fresh_keys, positives, write_slot):
    vmem = pl.BlockSpec(memory_space=pltpu.VMEM)
    loss, weight_grad, new_queue = pl.pallas_call(
        kernel,
        out_shape=(
            jax.ShapeDtypeStruct((1, 128), F32),
            jax.ShapeDtypeStruct((8, WIDTH), F32),
            jax.ShapeDtypeStruct((SLOT_ROWS, WIDTH), BF16),
        ),
        in_specs=[vmem] * 5 + [pl.BlockSpec(memory_space=pltpu.SMEM)],
        out_specs=(vmem, vmem, vmem),
        scratch_shapes=[
            pltpu.VMEM((4, ROWS, WIDTH), F32),
            pltpu.VMEM((3, ROWS, WIDTH), F32),
            pltpu.VMEM((X, Z, ROWS, WIDTH), BF16),
            pltpu.VMEM((8, SLOT_ROWS, WIDTH), BF16),
            pltpu.VMEM((Z, X, ROWS, WIDTH), BF16),
            pltpu.VMEM((2, 8, 128), jnp.int32),
            pltpu.VMEM((8, 4, ROWS, WIDTH), BF16),
            pltpu.VMEM((8, 4, ROWS, WIDTH), BF16),
            pltpu.VMEM((512, 128), BF16),
            pltpu.VMEM((3, Z, ROWS, WIDTH), BF16),
            pltpu.VMEM((3, Z, ROWS, WIDTH), BF16),
            pltpu.VMEM((Z, ROWS, WIDTH), BF16),
            pltpu.VMEM((7, ROWS, WIDTH), BF16),
            pltpu.VMEM((3, 8, 128), F32),
            pltpu.VMEM((3, 8, 128), F32),
            pltpu.VMEM((Z, 8, 128), F32),
            pltpu.VMEM((7, 8, 128), F32),
            pltpu.VMEM((4, ROWS, WIDTH), BF16),
            pltpu.VMEM((8, 128), F32),
            pltpu.VMEM((3, 8, 128), F32),
            pltpu.VMEM((Z, X, 16, WIDTH), F32),
            pltpu.VMEM((3, Z, 16, WIDTH), F32),
            pltpu.VMEM((Z, 16, WIDTH), F32),
            pltpu.VMEM((7, 16, WIDTH), F32),
            pltpu.VMEM((2, 8, WIDTH), F32),
            pltpu.VMEM((8, WIDTH), F32),
            pltpu.SemaphoreType.DMA((COPIES,)),
            pltpu.SemaphoreType.DMA((COPIES,)),
        ],
        compiler_params=pltpu.CompilerParams(
            collective_id=0, has_side_effects=True, vmem_limit_bytes=48 << 20
        ),
        name="retrieval_step",
    )(features, weight, queue, fresh_keys, positives.reshape(1, 128), write_slot)
    return loss.reshape(128), weight_grad, new_queue


def solution(mesh):
    in_specs = (
        P("blk", "group"),
        P("group", None),
        P(("group", "blk"), None),
        P("blk", None),
        P("blk"),
        P(),
    )
    out_specs = (P("blk"), P(("group", "blk"), None), P(("group", "blk"), None))
    return jax.shard_map(local, mesh=mesh, in_specs=in_specs, out_specs=out_specs, check_vma=False)
```

time: 666 us -> 78.7 us (0.12)
  waiting for transfers between devices: 496 us -> 0 us
  Pallas kernels: 0 us -> 70 us
  starting transfers between devices: 57 us -> 0 us
  matrix products: 41 us -> 0 us
  local copies, waits for them, and re-layouts: 28.9 us -> 6.1 us
  between operations: 14.9 us -> 1.3 us
  blocking collectives: 13.4 us -> 0 us
  other arithmetic: 12.5 us -> 0 us
    reduce_scatter x1 -> x0, waiting for transfers between devices: 334 us -> none  [in_one_piece_2(): whole = lax.psum_scatter(both, axis, scatter_dimension=dim, tiled=True)]
    all_gather x1 -> x0, waiting for transfers between devices: 146 us -> none  [in_one_piece(): lax.all_gather(both, axis, axis=dim, tiled=True)]
    pallas_call x0 -> x1, Pallas kernels: none -> 70 us  [local(): pl.pallas_call(kernel, out_shape=(jax.ShapeDtypeStruct((1, 128), F32), ja...]
    all_to_all x2 -> x0, starting transfers between devices: 56.9 us -> none  [the longest x1 51.7 us: from_everyone(): return lax.all_to_all(copies, axis, split_axis=0, concat_axis=0, tiled=True)]
    dot_general x34 -> x0, matrix products: 41 us -> none  [the longest x16 21 us: score_block(): jnp.einsum('qc,sc->qs', rows_now, queue, preferred_element_type=jnp.float32)]
    all_to_all x2 -> x0, waiting for transfers between devices: 15 us -> none  [the longest x1 10.7 us: sum_at_owner(): parts = lax.all_to_all(split_up(array, dim, length), axis, 0, 0, tiled=True)]
    all_to_all x1 -> x0, blocking collectives: 13.4 us -> none  [from_everyone(): return lax.all_to_all(copies, axis, split_axis=0, concat_axis=0, tiled=True)]
    reshape x3 -> x0, local copies, waits for them, and re-layouts: 9.64 us -> none  [the longest x1 8.93 us: local(): numer_all = numer_blocks.reshape(query_total, key_width)]
  transfers between devices with their start and end apart: 4 -> 0, of which waited for: 4 -> 0; matrix products, arithmetic and copies ran while one was open for 1% -> 0% of each run, Pallas kernels for 0% -> 0%
where the time goes in v1:
time: 78.7 us; the launch traced here: 77.4 us
  Pallas kernels  70 us (89%)
  local copies, waits for them, and re-layouts  6.1 us (8%)
  between operations  1.3 us (2%)
    pallas_call x1, Pallas kernels, local(): pl.pallas_call(kernel, out_shape=(jax.ShapeDtypeStruct((1, 128), F32), ja...  70 us
    unnamed x13, local copies, waits for them, and re-layouts  6.1 us

profile of v1, /device:TPU:1, one launch (start us, length us, event | category | flops | bytes accessed | tf_op | source)
XLA Modules:
  0.0 77.4 jit_solution(5055330704086678303)
XLA Ops:
  1.3 0.0 copy-start.4
  1.3 0.6 copy-done.4
  1.9 0.0 copy-start
  1.9 0.9 %copy-done = bf16[512,256]{1,0:T(8,128)(2,1)S(1)} copy-done((bf16[512,256]{1,0:T(8,128)(2,1)S(1)}, bf16[512,256]{1,0:T(8,128)(2,1)}, u32[]{:S(2)}) %copy-start) | copy-done | bytes 262168
  2.9 0.0 copy-start.1
  2.9 0.9 %copy-done.1 = bf16[512,256]{1,0:T(8,128)(2,1)S(1)} copy-done((bf16[512,256]{1,0:T(8,128)(2,1)S(1)}, bf16[512,256]{1,0:T(8,128)(2,1)}, u32[]{:S(2)}) %copy-start.1) | copy-done | bytes 262168
  3.8 0.0 copy-start.2
  3.8 0.9 %copy-done.2 = bf16[128,512]{1,0:T(8,128)(2,1)S(1)} copy-done((bf16[128,512]{1,0:T(8,128)(2,1)S(1)}, bf16[128,512]{1,0:T(8,128)(2,1)}, u32[]{:S(2)}) %copy-start.2) | copy-done | bytes 131096
  4.7 0.0 copy-start.3
  4.7 0.8 %copy-done.3 = bf16[128,256]{1,0:T(8,128)(2,1)S(1)} copy-done((bf16[128,256]{1,0:T(8,128)(2,1)S(1)}, bf16[128,256]{1,0:T(8,128)(2,1)}, u32[]{:S(2)}) %copy-start.3) | copy-done | bytes 65560
  5.6 70.0 %retrieval_step.1 = (f32[1,128]{1,0:T(1,128)S(1)}, f32[8,256]{1,0:T(8,128)S(1)}, bf16[512,256]{1,0:T(8,128)(2,1)S(1)}) custom-call(bf16[128,512]{1,0:T(8,128)(2,1)S(1)} %copy-done.2, bf16[512,256]{1,0:T(8,128)(2,1)S(1)} %copy-done, bf16[512,256]{1,0:T(8,128)(2,1)S(1)} %copy-done.1, bf16[128,256]{1,0:T(8,128)(2,1)S(1)} %copy-done.3, s32[1,128]{1,0:T(1,128)S(1)} %bitcast.2, ...), custom_call_target="tpu_custom_call" | custom-call | tf_op jit(solution)/shard_map/retrieval_step/pallas_call | solution.py:348
  75.6 0.5 copy.13
  76.1 0.6 copy.14
  76.7 0.7 copy.15
Async XLA Ops:
  1.3 0.7 copy-start.4
  1.9 0.9 %copy-start = (bf16[512,256]{1,0:T(8,128)(2,1)S(1)}, bf16[512,256]{1,0:T(8,128)(2,1)}, u32[]{:S(2)}) copy-start(bf16[512,256]{1,0:T(8,128)(2,1)} %weight.1) | copy-start | bytes 786436
  2.9 0.9 %copy-start.1 = (bf16[512,256]{1,0:T(8,128)(2,1)S(1)}, bf16[512,256]{1,0:T(8,128)(2,1)}, u32[]{:S(2)}) copy-start(bf16[512,256]{1,0:T(8,128)(2,1)} %queue.1) | copy-start | bytes 786436
  3.8 0.9 %copy-start.2 = (bf16[128,512]{1,0:T(8,128)(2,1)S(1)}, bf16[128,512]{1,0:T(8,128)(2,1)}, u32[]{:S(2)}) copy-start(bf16[128,512]{1,0:T(8,128)(2,1)} %features.1) | copy-start | bytes 393220
  4.7 0.8 %copy-start.3 = (bf16[128,256]{1,0:T(8,128)(2,1)S(1)}, bf16[128,256]{1,0:T(8,128)(2,1)}, u32[]{:S(2)}) copy-start(bf16[128,256]{1,0:T(8,128)(2,1)} %fresh.1) | copy-start | bytes 196612

commit v2 on v1

v2 whole, which is shorter than its diff:
```python
import functools
import math

import jax
import jax.numpy as jnp
from jax import lax
from jax.experimental import pallas as pl
from jax.experimental.pallas import tpu as pltpu
from jax.sharding import PartitionSpec as P

EPSILON = 1e-06
SHARP = 8.0
SHARP_LOG2E = SHARP * math.log2(math.e)

Z, X, Y, CORES = 8, 4, 4, 2
ROWS = 32
WIDTH = 256
SLOT_ROWS = 512
QUERIES = 8192
F32 = jnp.float32
BF16 = jnp.bfloat16
COPIES = 128


def lane_sums(e):
    d = e[:, 0:128]
    for i in range(1, e.shape[1] // 128):
        d = d + e[:, 128 * i : 128 * (i + 1)]
    return d


def kernel(
    features_hbm,
    weight_hbm,
    queue_hbm,
    fresh_hbm,
    positives_hbm,
    write_slot,
    loss_out,
    wgrad_out,
    queue_out,
    features,
    weight,
    proj,
    proj_in,
    queries,
    keys,
    fresh_all,
    pos_row,
    pos_all,
    pick_out,
    pick_in,
    fill_out,
    fill_in,
    feat_t,
    num_own,
    num_out,
    num_in,
    numz_out,
    numz_in,
    den_own,
    den_out,
    den_in,
    denz_out,
    denz_in,
    gp_all,
    loss_rows,
    loss_in,
    wg,
    wg_out,
    wg_in,
    wgz_out,
    wgz_in,
    local_sem,
    send_sem,
    recv_sem,
):
    g = lax.axis_index("group")
    b = lax.axis_index("blk")
    y_lo, c = g // 2, g % 2
    z, x, y_hi = b // 8, (b // 2) % 4, b % 2
    y = 2 * y_hi + y_lo
    me_col = y * 2 + c

    loads = [
        pltpu.make_async_copy(src, dst, local_sem.at[i])
        for i, (src, dst) in enumerate(
            (
                (features_hbm, features),
                (weight_hbm, weight),
                (queue_hbm, keys.at[me_col]),
                (fresh_hbm.at[pl.ds(pl.multiple_of(g * ROWS, ROWS), ROWS)], fresh_all.at[z, x]),
                (positives_hbm, pos_row),
            )
        )
    ]
    for copy in loads:
        copy.start()

    def device(zz, xx, yy, cc):
        return {"group": (yy % 2) * 2 + cc, "blk": zz * 8 + xx * 2 + yy // 2}

    started = []

    def send(src, dst, to):
        at = len(started)
        copy = pltpu.make_async_remote_copy(
            src_ref=src,
            dst_ref=dst,
            send_sem=send_sem.at[at],
            recv_sem=recv_sem.at[at],
            device_id=to,
            device_id_type=pl.DeviceIdType.MESH,
        )
        copy.start()
        started.append(copy)
        return copy

    column = [(dy, dc) for dy in (0, 1, 3, 2) for dc in (1, 0) if (dy, dc) != (0, 0)]
    z_order = (1, 7, 2, 6, 3, 5, 4)
    x_order = (1, 3, 2)
    rect = [(dx, dy) for dx in (1, 3, 2, 0) for dy in (2, 0) if (dx, dy) != (0, 0)]

    barrier = pltpu.get_barrier_semaphore()
    peers = [device((z + d) % 8, x, y, c) for d in z_order]
    peers += [device(z, x, (y + dy) % 4, (c + dc) % 2) for dy, dc in column]
    peers += [device(z, (x + dx) % 4, (y + dy) % 4, c) for dx, dy in rect if dx]
    for p in peers:
        pl.semaphore_signal(barrier, inc=1, device_id=p, device_id_type=pl.DeviceIdType.MESH)

    for copy in loads:
        copy.wait()
    proj[...] = jnp.dot(features[...], weight[...], preferred_element_type=F32).reshape(
        4, ROWS, WIDTH
    )
    pos_all[0] = jnp.broadcast_to(pos_row[...], (8, 128))
    pl.semaphore_wait(barrier, len(peers))

    group_peers = []
    for s in (1, 2, 3):
        yy, cc = 2 * y_hi + (y_lo + s // 2) % 2, (c + s % 2) % 2
        group_peers.append((s, yy, cc))
    proj_copies = [
        send(proj.at[(yy % 2) * 2 + cc], proj_in.at[s - 1], device(z, x, yy, cc))
        for s, yy, cc in group_peers
    ]

    up, down = (y + 1) % 4, (y + 3) % 4
    far = (y + 2) % 4
    other = 1 - c
    to_up, to_down = device(z, x, up, c), device(z, x, down, c)
    to_other = device(z, x, y, other)
    half = SLOT_ROWS // 2

    def part(yy, h):
        return keys.at[yy * 2 + c, pl.ds(h * half, half)]

    def pass_on(yy, h, to):
        return send(part(yy, h), part(yy, h), to)

    up_low = pass_on(y, 0, to_up)
    down_high = pass_on(y, 1, to_down)
    key_other = [pass_on(y, h, to_other) for h in range(2)]
    up_high = pass_on(y, 1, to_up)
    down_low = pass_on(y, 0, to_down)
    pos_copy = send(pos_all.at[0], pos_all.at[1], device(z, x, far, c))

    for copy in proj_copies:
        copy.wait_recv()
    projected = proj[g] + proj_in[0] + proj_in[1] + proj_in[2]
    length = jnp.sqrt(jnp.sum(projected * projected, axis=1, keepdims=True) + EPSILON)
    unit = projected / length
    query = unit.astype(BF16)
    queries[x, z] = query
    own_q = queries.at[x, z]
    qz = {d: send(own_q, own_q, device((z + d) % 8, x, y, c)) for d in z_order}
    qx = {(d, 0): send(own_q, own_q, device(z, (x + d) % 4, y, c)) for d in x_order}
    own_f = fresh_all.at[z, x]
    fz = [send(own_f, own_f, device((z + d) % 8, x, y, c)) for d in z_order]
    feat_t[...] = features[...].T

    up_low.wait_recv()
    far_low = pass_on(down, 0, to_up)
    key_other.append(pass_on(down, 0, to_other))
    down_high.wait_recv()
    far_high = pass_on(up, 1, to_down)
    key_other.append(pass_on(up, 1, to_other))
    for d in z_order:
        qz[d].wait_recv()
        block = queries.at[x, (z + 8 - d) % 8]
        for e in x_order:
            qx[e, d] = send(block, block, device(z, (x + e) % 4, y, c))
    up_high.wait_recv()
    key_other.append(pass_on(down, 1, to_other))
    down_low.wait_recv()
    key_other.append(pass_on(up, 0, to_other))
    for copy in key_other:
        copy.wait_recv()

    diagonal = lax.broadcasted_iota(jnp.int32, (ROWS, 128), 0) == lax.broadcasted_iota(
        jnp.int32, (ROWS, 128), 1
    )

    def tile(xx, where, num=None, den=None):
        q = queries[xx].reshape(Z * ROWS, WIDTH)
        for j in where:
            k = keys[j]
            s = lax.dot_general(q, k, (((1,), (1,)), ((), ())), preferred_element_type=F32)
            e = jnp.exp2(s * SHARP_LOG2E)
            p = jnp.dot(e.astype(BF16), k, preferred_element_type=F32)
            sums = lane_sums(e)
            num = p if num is None else num + p
            den = sums if den is None else den + sums
        return num, den

    def den_rows(den):
        column_sums = jnp.sum(den, axis=1, keepdims=True).reshape(Z, ROWS, 1)
        return jnp.sum(jnp.where(diagonal[None], column_sums, 0.0), axis=1)

    num_own[...], den_own[...] = tile(x, [yy * 2 + cc for yy in (y, down, up) for cc in (0, 1)])
    far_low.wait_recv()
    far_other = [pass_on(far, 0, to_other)]
    far_high.wait_recv()
    far_other.append(pass_on(far, 1, to_other))

    num_copies, den_copies = [], []

    def foreign_tile(i):
        d = x_order[i]
        for dz in (0, *z_order):
            qx[d, dz].wait_recv()
        if i == 0:
            for copy in far_other:
                copy.wait_recv()
        owner = (x + 4 - d) % 4
        num, den = tile(owner, range(8))
        num_out[i] = num.astype(BF16).reshape(Z, ROWS, WIDTH)
        den_out[i] = den_rows(den)
        to = device(z, owner, y, c)
        den_copies.append(send(den_out.at[i], den_in.at[i], to))
        num_copies.append(send(num_out.at[i], num_in.at[i], to))

    for copy in fz:
        copy.wait_recv()
    fresh_line = fresh_all.at[:, x]
    fx = [send(fresh_line, fresh_line, device(z, (x + d) % 4, y, c)) for d in x_order]
    foreign_tile(0)
    foreign_tile(1)

    for copy in fx:
        copy.wait_recv()
    pos_copy.wait_recv()
    held = fresh_all[...].reshape(Z * X * ROWS, WIDTH)
    lane = lax.broadcasted_iota(jnp.int32, (128, 128), 1)
    first_key = (lax.shift_right_logical(lane, 5) * 256 + (lane & 31) + me_col * ROWS).astype(F32)
    for r in range(2):
        wanted = jnp.broadcast_to(pos_all[r, 0:1, :], (128, 128)).astype(F32).T - first_key
        hits = [jnp.where(wanted == 1024.0 * m, 1.0, 0.0).astype(BF16) for m in range(8)]
        found = jnp.dot(jnp.concatenate(hits, axis=1), held, preferred_element_type=F32)
        found = found.astype(BF16).reshape(4, ROWS, WIDTH)
        for gg in range(4):
            pick_out[((y_hi + r) % 2) * 4 + gg] = found[gg]
    picks = []
    for dy, dc in column:
        yy, cc = (y + dy) % 4, (c + dc) % 2
        picks.append(send(pick_out.at[yy * 2 + cc], pick_in.at[me_col], device(z, x, yy, cc)))
    pick_in[me_col] = pick_out[me_col]
    foreign_tile(2)

    num, den = tile(x, [far * 2, far * 2 + 1], num_own[...], den_own[...])
    num, den = num.reshape(Z, ROWS, WIDTH), den_rows(den)
    for i in range(3):
        den_copies[i].wait_recv()
        den = den + den_in[i]
        num_copies[i].wait_recv()
        num = num + num_in[i].astype(F32)
    numz_out[...] = num.astype(BF16)
    denz_out[...] = jnp.broadcast_to(den[:, None, :], (Z, 8, 128))
    numz, denz = [], []
    for i, d in enumerate(z_order):
        zz = (z + d) % 8
        to = device(zz, x, y, c)
        denz.append(send(denz_out.at[zz], denz_in.at[i], to))
        numz.append(send(numz_out.at[zz], numz_in.at[i], to))

    slot = write_slot[0]

    def window(gg, bb):
        first = (gg * 64 + bb) * SLOT_ROWS - slot
        return first, lax.shift_right_arithmetic(first, 8)

    for target in range(8):
        _, cycle = window(target % 4, z * 8 + x * 2 + target // 4)
        for k in range(3):
            at = jnp.clip(cycle + k, 0, QUERIES // 256 - 1)
            fill_out[target, k] = fresh_all[lax.shift_right_logical(at, 2), at & 3]
    fills = []
    for dy, dc in column:
        yy, cc = (y + dy) % 4, (c + dc) % 2
        to = device(z, x, yy, cc)
        fills.append(send(fill_out.at[yy * 2 + cc], fill_in.at[:, me_col], to))
    fill_in[:, me_col] = fill_out[me_col]

    for copy in picks:
        copy.wait_recv()
    positive = pick_in[0].astype(F32)
    for src in range(1, 8):
        positive = positive + pick_in[src].astype(F32)
    score = SHARP * jnp.sum(query.astype(F32) * positive, axis=1, keepdims=True)
    weight_p = jnp.exp(score)

    numerator = numz_out[z].astype(F32)
    den_row = denz_out[z]
    for i in range(7):
        denz[i].wait_recv()
        den_row = den_row + denz_in[i]
        numz[i].wait_recv()
        numerator = numerator + numz_in[i].astype(F32)
    denominator = jnp.sum(
        jnp.where(diagonal, jnp.broadcast_to(den_row[0:1, :], (ROWS, 128)), 0.0),
        axis=1,
        keepdims=True,
    )
    mass = weight_p + denominator
    grad = SHARP * ((weight_p * positive + numerator) / mass - positive)
    along = jnp.sum(grad * unit, axis=1, keepdims=True)
    grad_projected = ((grad - along * unit) / length).astype(BF16)
    gp_all[g] = grad_projected
    gps = [send(gp_all.at[g], gp_all.at[g], device(z, x, yy, cc)) for _, yy, cc in group_peers]
    loss = jnp.log(mass) - score
    place = lax.broadcasted_iota(jnp.int32, (ROWS, 128), 0) + g * ROWS == (
        lax.broadcasted_iota(jnp.int32, (ROWS, 128), 1)
    )
    loss_row = jnp.sum(jnp.where(place, loss, 0.0), axis=0, keepdims=True)
    loss_rows[...] = jnp.broadcast_to(loss_row, (8, 128))
    losses = [
        send(loss_rows, loss_in.at[s - 1], device(z, x, yy, cc)) for s, yy, cc in group_peers
    ]
    for copy in gps:
        copy.wait_recv()
    grads = jnp.dot(feat_t[...], gp_all[...].reshape(128, WIDTH), preferred_element_type=F32)
    grads = grads.reshape(Z, X, 2, 8, WIDTH)
    for xx in range(X):
        for h in range(2):
            block = grads[:, xx, h].reshape(Z * 8, WIDTH)
            wg[xx * 2 + h] = block
            wg_out[xx * 2 + h] = block.astype(BF16)
    wgx = []
    for i, (dx, dy) in enumerate(rect):
        xx, yy = (x + dx) % 4, (y + dy) % 4
        wgx.append(send(wg_out.at[xx * 2 + yy // 2], wg_in.at[i], device(z, xx, yy, c)))

    for copy in fills:
        copy.wait_recv()
    first, cycle = window(g, b)
    arrived = fill_in[...].reshape(768, WIDTH)
    row = lax.broadcasted_iota(jnp.int32, (128, 128), 0)
    apart = row - lane + (first - cycle * 256)
    hit = [jnp.where(apart == 128 * m, 1.0, 0.0).astype(BF16) for m in range(3)]
    hit = jnp.concatenate(hit, axis=1)
    place_of = lax.broadcasted_iota(jnp.int32, (128, WIDTH), 0) + first
    for r in range(0, SLOT_ROWS, 128):
        moved = jnp.dot(hit, arrived[r : r + 384], preferred_element_type=F32)
        old = keys[me_col, r : r + 128, :].astype(F32)
        inside = (place_of >= -r) & (place_of < QUERIES - r)
        queue_out[r : r + 128, :] = jnp.where(inside, moved, old).astype(BF16)
    for copy in losses:
        copy.wait_recv()
    loss_out[...] = (loss_rows[...] + loss_in[0] + loss_in[1] + loss_in[2])[0:1, :]

    sums = wg[x * 2 + y_hi]
    for i, copy in enumerate(wgx):
        copy.wait_recv()
        sums = sums + wg_in[i].astype(F32)
    wgz_out[...] = sums.reshape(Z, 8, WIDTH)
    wgz = []
    for i, d in enumerate(z_order):
        zz = (z + d) % 8
        wgz.append(send(wgz_out.at[zz], wgz_in.at[i], device(zz, x, y, c)))
    total = wgz_out[z]
    for i in range(7):
        wgz[i].wait_recv()
        total = total + wgz_in[i]
    wgrad_out[...] = total

    for copy in started:
        copy.wait_send()


def local(features, weight, queue, fresh_keys, positives, write_slot):
    vmem = pl.BlockSpec(memory_space=pltpu.VMEM)
    loss, weight_grad, new_queue = pl.pallas_call(
        kernel,
        out_shape=(
            jax.ShapeDtypeStruct((1, 128), F32),
            jax.ShapeDtypeStruct((8, WIDTH), F32),
            jax.ShapeDtypeStruct((SLOT_ROWS, WIDTH), BF16),
        ),
        in_specs=[pl.BlockSpec(memory_space=pltpu.HBM)] * 5
        + [pl.BlockSpec(memory_space=pltpu.SMEM)],
        out_specs=(vmem, vmem, vmem),
        scratch_shapes=[
            pltpu.VMEM((128, 512), BF16),
            pltpu.VMEM((512, WIDTH), BF16),
            pltpu.VMEM((4, ROWS, WIDTH), F32),
            pltpu.VMEM((3, ROWS, WIDTH), F32),
            pltpu.VMEM((X, Z, ROWS, WIDTH), BF16),
            pltpu.VMEM((8, SLOT_ROWS, WIDTH), BF16),
            pltpu.VMEM((Z, X, ROWS, WIDTH), BF16),
            pltpu.VMEM((1, 128), jnp.int32),
            pltpu.VMEM((2, 8, 128), jnp.int32),
            pltpu.VMEM((8, ROWS, WIDTH), BF16),
            pltpu.VMEM((8, ROWS, WIDTH), BF16),
            pltpu.VMEM((8, 3, ROWS, WIDTH), BF16),
            pltpu.VMEM((3, 8, ROWS, WIDTH), BF16),
            pltpu.VMEM((512, 128), BF16),
            pltpu.VMEM((Z * ROWS, WIDTH), F32),
            pltpu.VMEM((3, Z, ROWS, WIDTH), BF16),
            pltpu.VMEM((3, Z, ROWS, WIDTH), BF16),
            pltpu.VMEM((Z, ROWS, WIDTH), BF16),
            pltpu.VMEM((7, ROWS, WIDTH), BF16),
            pltpu.VMEM((Z * ROWS, 128), F32),
            pltpu.VMEM((3, 8, 128), F32),
            pltpu.VMEM((3, 8, 128), F32),
            pltpu.VMEM((Z, 8, 128), F32),
            pltpu.VMEM((7, 8, 128), F32),
            pltpu.VMEM((4, ROWS, WIDTH), BF16),
            pltpu.VMEM((8, 128), F32),
            pltpu.VMEM((3, 8, 128), F32),
            pltpu.VMEM((8, Z * 8, WIDTH), F32),
            pltpu.VMEM((8, Z * 8, WIDTH), BF16),
            pltpu.VMEM((7, Z * 8, WIDTH), BF16),
            pltpu.VMEM((Z, 8, WIDTH), F32),
            pltpu.VMEM((7, 8, WIDTH), F32),
            pltpu.SemaphoreType.DMA((5,)),
            pltpu.SemaphoreType.DMA((COPIES,)),
            pltpu.SemaphoreType.DMA((COPIES,)),
        ],
        compiler_params=pltpu.CompilerParams(
            collective_id=0, has_side_effects=True, vmem_limit_bytes=48 << 20
        ),
        name="retrieval_step",
    )(features, weight, queue, fresh_keys, positives.reshape(1, 128), write_slot)
    return loss.reshape(128), weight_grad, new_queue


def solution(mesh):
    in_specs = (
        P("blk", "group"),
        P("group", None),
        P(("group", "blk"), None),
        P("blk", None),
        P("blk"),
        P(),
    )
    out_specs = (P("blk"), P(("group", "blk"), None), P(("group", "blk"), None))
    return jax.shard_map(local, mesh=mesh, in_specs=in_specs, out_specs=out_specs, check_vma=False)
```

time: 78.7 us -> 68.7 us (0.87)
  Pallas kernels: 70 us -> 60.8 us
    pallas_call x1, Pallas kernels: 70 us -> 60.8 us  [local(): pl.pallas_call(kernel, out_shape=(jax.ShapeDtypeStruct((1, 128), F32), ja...]
where the time goes in v2:
time: 68.7 us; the launch traced here: 68.2 us
  Pallas kernels  60.8 us (89%)
  local copies, waits for them, and re-layouts  6.1 us (9%)
  between operations  1.3 us (2%)
    pallas_call x1, Pallas kernels, local(): pl.pallas_call(kernel, out_shape=(jax.ShapeDtypeStruct((1, 128), F32), ja...  60.8 us
    unnamed x13, local copies, waits for them, and re-layouts  6.1 us

profile of v2, /device:TPU:1, one launch (start us, length us, event | category | flops | bytes accessed | tf_op | source)
XLA Modules:
  0.0 68.2 jit_solution(17414491783420441177)
XLA Ops:
  1.3 0.0 copy-start.4
  1.3 0.6 copy-done.4
  1.9 0.0 copy-start
  1.9 0.9 %copy-done = bf16[512,256]{1,0:T(8,128)(2,1)S(1)} copy-done((bf16[512,256]{1,0:T(8,128)(2,1)S(1)}, bf16[512,256]{1,0:T(8,128)(2,1)}, u32[]{:S(2)}) %copy-start) | copy-done | bytes 262168
  2.9 0.0 copy-start.1
  2.9 0.9 %copy-done.1 = bf16[512,256]{1,0:T(8,128)(2,1)S(1)} copy-done((bf16[512,256]{1,0:T(8,128)(2,1)S(1)}, bf16[512,256]{1,0:T(8,128)(2,1)}, u32[]{:S(2)}) %copy-start.1) | copy-done | bytes 262168
  3.8 0.0 copy-start.2
  3.8 0.9 %copy-done.2 = bf16[128,512]{1,0:T(8,128)(2,1)S(1)} copy-done((bf16[128,512]{1,0:T(8,128)(2,1)S(1)}, bf16[128,512]{1,0:T(8,128)(2,1)}, u32[]{:S(2)}) %copy-start.2) | copy-done | bytes 131096
  4.7 0.0 copy-start.3
  4.7 0.8 %copy-done.3 = bf16[128,256]{1,0:T(8,128)(2,1)S(1)} copy-done((bf16[128,256]{1,0:T(8,128)(2,1)S(1)}, bf16[128,256]{1,0:T(8,128)(2,1)}, u32[]{:S(2)}) %copy-start.3) | copy-done | bytes 65560
  5.6 60.8 %retrieval_step.1 = (f32[1,128]{1,0:T(1,128)S(1)}, f32[8,256]{1,0:T(8,128)S(1)}, bf16[512,256]{1,0:T(8,128)(2,1)S(1)}) custom-call(bf16[128,512]{1,0:T(8,128)(2,1)S(1)} %copy-done.2, bf16[512,256]{1,0:T(8,128)(2,1)S(1)} %copy-done, bf16[512,256]{1,0:T(8,128)(2,1)S(1)} %copy-done.1, bf16[128,256]{1,0:T(8,128)(2,1)S(1)} %copy-done.3, s32[1,128]{1,0:T(1,128)S(1)} %bitcast.2, ...), custom_call_target="tpu_custom_call" | custom-call | tf_op jit(solution)/shard_map/retrieval_step/pallas_call | solution.py:392
  66.4 0.5 copy.13
  66.9 0.6 copy.14
  67.5 0.7 %copy.15 = bf16[512,256]{1,0:T(8,128)(2,1)} copy(bf16[512,256]{1,0:T(8,128)(2,1)S(1)} %get-tuple-element.14) | data formatting | bytes 524288
Async XLA Ops:
  1.3 0.7 copy-start.4
  1.9 0.9 %copy-start = (bf16[512,256]{1,0:T(8,128)(2,1)S(1)}, bf16[512,256]{1,0:T(8,128)(2,1)}, u32[]{:S(2)}) copy-start(bf16[512,256]{1,0:T(8,128)(2,1)} %weight_hbm.1) | copy-start | bytes 786436
  2.9 0.9 %copy-start.1 = (bf16[512,256]{1,0:T(8,128)(2,1)S(1)}, bf16[512,256]{1,0:T(8,128)(2,1)}, u32[]{:S(2)}) copy-start(bf16[512,256]{1,0:T(8,128)(2,1)} %queue_hbm.1) | copy-start | bytes 786436
  3.8 0.9 %copy-start.2 = (bf16[128,512]{1,0:T(8,128)(2,1)S(1)}, bf16[128,512]{1,0:T(8,128)(2,1)}, u32[]{:S(2)}) copy-start(bf16[128,512]{1,0:T(8,128)(2,1)} %features_hbm.1) | copy-start | bytes 393220
  4.7 0.8 %copy-start.3 = (bf16[128,256]{1,0:T(8,128)(2,1)S(1)}, bf16[128,256]{1,0:T(8,128)(2,1)}, u32[]{:S(2)}) copy-start(bf16[128,256]{1,0:T(8,128)(2,1)} %fresh_hbm.1) | copy-start | bytes 196612

commit v3 on v2

v3 whole, which is shorter than its diff:
```python
import functools
import math

import jax
import jax.numpy as jnp
from jax import lax
from jax.experimental import pallas as pl
from jax.experimental.pallas import tpu as pltpu
from jax.sharding import PartitionSpec as P

EPSILON = 1e-06
SHARP = 8.0
SHARP_LOG2E = SHARP * math.log2(math.e)

Z, X, Y, CORES = 8, 4, 4, 2
ROWS = 32
WIDTH = 256
SLOT_ROWS = 512
QUERIES = 8192
F32 = jnp.float32
BF16 = jnp.bfloat16
COPIES = 47


def lane_sums(e):
    d = e[:, 0:128]
    for i in range(1, e.shape[1] // 128):
        d = d + e[:, 128 * i : 128 * (i + 1)]
    return d


def kernel(
    features_hbm,
    weight_hbm,
    queue_hbm,
    fresh_hbm,
    positives_hbm,
    write_slot,
    loss_out,
    wgrad_out,
    queue_out,
    features,
    weight,
    proj,
    proj_in,
    queries,
    keys,
    fresh_all,
    pos_row,
    pos_all,
    pick_out,
    pick_in,
    fill_out,
    fill_in,
    feat_t,
    num_own,
    num_out,
    num_in,
    num_far_out,
    num_far_in,
    num_sum_out,
    num_sum_in,
    numz_out,
    numz_in,
    den_own,
    den_out,
    den_in,
    den_far_out,
    den_far_in,
    den_sum_out,
    den_sum_in,
    denz_out,
    denz_in,
    gp_all,
    loss_rows,
    loss_in,
    wg,
    wg_out,
    wg_in,
    wgz_out,
    wgz_in,
    queue_new,
    loss_new,
    wgrad_new,
    local_sem,
    send_sem,
    recv_sem,
):
    g = lax.axis_index("group")
    b = lax.axis_index("blk")
    y_lo, c = g // 2, g % 2
    z, x, y_hi = b // 8, (b // 2) % 4, b % 2
    y = 2 * y_hi + y_lo
    me_col = y * 2 + c

    loads = [
        pltpu.make_async_copy(src, dst, local_sem.at[i])
        for i, (src, dst) in enumerate(
            (
                (features_hbm, features),
                (weight_hbm, weight),
                (queue_hbm, keys.at[me_col]),
                (fresh_hbm.at[pl.ds(pl.multiple_of(g * ROWS, ROWS), ROWS)], fresh_all.at[z, x]),
                (positives_hbm, pos_row),
            )
        )
    ]
    for copy in loads:
        copy.start()

    def device(zz, xx, yy, cc):
        return {"group": (yy % 2) * 2 + cc, "blk": zz * 8 + xx * 2 + yy // 2}

    groups = []

    class Group:
        def __init__(self, whole):
            self.at, self.whole, self.got = len(groups), whole, False
            groups.append(self)

        def copy(self, src, dst, to):
            return pltpu.make_async_remote_copy(
                src_ref=src,
                dst_ref=dst,
                send_sem=send_sem.at[self.at],
                recv_sem=recv_sem.at[self.at],
                device_id=to,
                device_id_type=pl.DeviceIdType.MESH,
            )

        def send(self, src, dst, to):
            self.copy(src, dst, to).start()

        def wait_recv(self):
            self.got = True
            self.copy(self.whole, self.whole, neighbour).wait_recv()

        def wait_send(self):
            self.copy(self.whole, self.whole, neighbour).wait_send()

    neighbour = device(z, x, y, 1 - c)

    def send(src, dst, to):
        group = Group(src)
        group.send(src, dst, to)
        return group

    column = [(dy, dc) for dy in (0, 1, 3, 2) for dc in (1, 0) if (dy, dc) != (0, 0)]
    z_order = (1, 7, 2, 6, 3, 5, 4)
    z_far = (4, 3, 5, 2, 6, 1, 7)
    rect = [(dx, dy) for dx in (2, 1, 3, 0) for dy in (2, 0) if (dx, dy) != (0, 0)]
    x_near, x_far = (x + 1) % 4, (x + 2) % 4
    x_back = (x + 3) % 4

    barrier = pltpu.get_barrier_semaphore()
    peers = [device((z + d) % 8, x, y, c) for d in z_far]
    peers += [device(z, x, (y + dy) % 4, (c + dc) % 2) for dy, dc in column]
    peers += [device(z, (x + dx) % 4, (y + dy) % 4, c) for dx, dy in rect if dx]
    for p in peers:
        pl.semaphore_signal(barrier, inc=1, device_id=p, device_id_type=pl.DeviceIdType.MESH)

    for copy in loads:
        copy.wait()
    proj[...] = jnp.dot(features[...], weight[...], preferred_element_type=F32).reshape(
        4, ROWS, WIDTH
    )
    pos_all[0] = jnp.broadcast_to(pos_row[...], (8, 128))
    pl.semaphore_wait(barrier, len(peers))

    group_peers = []
    for s in (1, 2, 3):
        yy, cc = 2 * y_hi + (y_lo + s // 2) % 2, (c + s % 2) % 2
        group_peers.append((s, yy, cc))
    proj_copies = Group(proj_in)
    for s, yy, cc in group_peers:
        proj_copies.send(proj.at[(yy % 2) * 2 + cc], proj_in.at[s - 1], device(z, x, yy, cc))

    own_f = fresh_all.at[z, x]
    fz = Group(fresh_all.at[pl.ds(0, 7), x])
    fresh_far = send(own_f, own_f, device(z, x_far, y, c))
    for d in z_order:
        fz.send(own_f, own_f, device((z + d) % 8, x, y, c))

    up, down = (y + 1) % 4, (y + 3) % 4
    far = (y + 2) % 4
    other = 1 - c
    to_up, to_down = device(z, x, up, c), device(z, x, down, c)
    to_other = device(z, x, y, other)
    half = SLOT_ROWS // 2

    def part(yy, h):
        return keys.at[yy * 2 + c, pl.ds(h * half, half)]

    def pass_on(yy, h, to):
        return send(part(yy, h), part(yy, h), to)

    up_low = pass_on(y, 0, to_up)
    down_high = pass_on(y, 1, to_down)
    key_other = [pass_on(y, h, to_other) for h in range(2)]
    up_high = pass_on(y, 1, to_up)
    down_low = pass_on(y, 0, to_down)
    pos_copy = send(pos_all.at[0], pos_all.at[1], device(z, x, far, c))

    proj_copies.wait_recv()
    projected = proj[g] + proj_in[0] + proj_in[1] + proj_in[2]
    length = jnp.sqrt(jnp.sum(projected * projected, axis=1, keepdims=True) + EPSILON)
    unit = projected / length
    query = unit.astype(BF16)
    queries[x, z] = query
    own_q = queries.at[x, z]
    qx = {d: Group(queries.at[x]) for d in (1, 3)}
    query_far = send(own_q, own_q, device(z, x_far, y, c))
    qz = {d: send(own_q, own_q, device((z + d) % 8, x, y, c)) for d in z_order}
    for d in (1, 3):
        qx[d].send(own_q, own_q, device(z, (x + d) % 4, y, c))
    fresh_far.wait_recv()
    block = fresh_all.at[z, x_far]
    fz_far = Group(fresh_all.at[pl.ds(0, 7), x])
    for d in z_order:
        fz_far.send(block, block, device((z + d) % 8, x, y, c))
    fz.wait_recv()
    fresh_line = fresh_all.at[:, x]
    fx = Group(fresh_all.at[:, pl.ds(0, 2)])
    for xx in (x_near, x_back):
        fx.send(fresh_line, fresh_line, device(z, xx, y, c))
    feat_t[...] = features[...].T

    up_low.wait_recv()
    far_low = pass_on(down, 0, to_up)
    key_other.append(pass_on(down, 0, to_other))
    down_high.wait_recv()
    far_high = pass_on(up, 1, to_down)
    key_other.append(pass_on(up, 1, to_other))
    query_far.wait_recv()
    block = queries.at[x_far, z]
    qz_far = Group(queries.at[x, pl.ds(0, 7)])
    for d in z_order:
        qz_far.send(block, block, device((z + d) % 8, x, y, c))
    for d in z_order:
        qz[d].wait_recv()
        block = queries.at[x, (z + 8 - d) % 8]
        for e in (1, 3):
            qx[e].send(block, block, device(z, (x + e) % 4, y, c))
    up_high.wait_recv()
    key_other.append(pass_on(down, 1, to_other))
    down_low.wait_recv()
    key_other.append(pass_on(up, 0, to_other))
    for copy in key_other:
        copy.wait_recv()

    diagonal = lax.broadcasted_iota(jnp.int32, (ROWS, 128), 0) == lax.broadcasted_iota(
        jnp.int32, (ROWS, 128), 1
    )

    def tile(xx, where, num=None, den=None):
        q = queries[xx].reshape(Z * ROWS, WIDTH)
        for j in where:
            k = keys[j]
            s = lax.dot_general(q, k, (((1,), (1,)), ((), ())), preferred_element_type=F32)
            e = jnp.exp2(s * SHARP_LOG2E)
            p = jnp.dot(e.astype(BF16), k, preferred_element_type=F32)
            sums = lane_sums(e)
            num = p if num is None else num + p
            den = sums if den is None else den + sums
        return num, den

    def den_rows(den):
        column_sums = jnp.sum(den, axis=1, keepdims=True).reshape(Z, ROWS, 1)
        return jnp.sum(jnp.where(diagonal[None], column_sums, 0.0), axis=1)

    num_own[...], den_own[...] = tile(x, [yy * 2 + cc for yy in (y, down, up) for cc in (0, 1)])
    far_low.wait_recv()
    far_other = [pass_on(far, 0, to_other)]
    far_high.wait_recv()
    far_other.append(pass_on(far, 1, to_other))

    fz_far.wait_recv()
    fx.wait_recv()
    pos_copy.wait_recv()
    held = fresh_all[...].reshape(Z * X * ROWS, WIDTH)
    lane = lax.broadcasted_iota(jnp.int32, (128, 128), 1)
    first_key = (lax.shift_right_logical(lane, 5) * 256 + (lane & 31) + me_col * ROWS).astype(F32)
    for r in range(2):
        wanted = jnp.broadcast_to(pos_all[r, 0:1, :], (128, 128)).astype(F32).T - first_key
        hits = [jnp.where(wanted == 1024.0 * m, 1.0, 0.0).astype(BF16) for m in range(8)]
        found = jnp.dot(jnp.concatenate(hits, axis=1), held, preferred_element_type=F32)
        found = found.astype(BF16).reshape(4, ROWS, WIDTH)
        for gg in range(4):
            pick_out[((y_hi + r) % 2) * 4 + gg] = found[gg]
    picks = Group(pick_in.at[pl.ds(0, 7)])
    for dy, dc in column:
        yy, cc = (y + dy) % 4, (c + dc) % 2
        picks.send(pick_out.at[yy * 2 + cc], pick_in.at[me_col], device(z, x, yy, cc))
    pick_in[me_col] = pick_out[me_col]

    slot = write_slot[0]

    def window(gg, bb):
        first = (gg * 64 + bb) * SLOT_ROWS - slot
        return first, lax.shift_right_arithmetic(first, 8)

    for target in range(8):
        _, cycle = window(target % 4, z * 8 + x * 2 + target // 4)
        for k in range(3):
            at = jnp.clip(cycle + k, 0, QUERIES // 256 - 1)
            fill_out[target, k] = fresh_all[lax.shift_right_logical(at, 2), at & 3]
    fills = Group(fill_in.at[:, pl.ds(0, 7)])
    for dy, dc in column:
        yy, cc = (y + dy) % 4, (c + dc) % 2
        to = device(z, x, yy, cc)
        fills.send(fill_out.at[yy * 2 + cc], fill_in.at[:, me_col], to)
    fill_in[:, me_col] = fill_out[me_col]

    for copy in far_other:
        copy.wait_recv()
    num_copies, den_copies = [], []
    for i, d in enumerate((1, 3)):
        qx[d].wait_recv()
        owner = (x + 4 - d) % 4
        num, den = tile(owner, range(8))
        num_out[i] = num.astype(BF16).reshape(Z, ROWS, WIDTH)
        den_out[i] = den_rows(den)
        to = device(z, owner, y, c)
        den_copies.append(send(den_out.at[i], den_in.at[i], to))
        num_copies.append(send(num_out.at[i], num_in.at[i], to))
    qz_far.wait_recv()
    num, den = tile(x_far, range(8))
    num_far_out[...] = num.astype(BF16).reshape(Z, ROWS, WIDTH)
    den_far_out[...] = den_rows(den).reshape(Z, 1, 128)
    numf, denf = Group(num_far_in), Group(den_far_in)
    for i, d in enumerate(z_far):
        zz = (z + d) % 8
        to = device(zz, x, y, c)
        denf.send(den_far_out.at[zz], den_far_in.at[i], to)
        numf.send(num_far_out.at[zz], num_far_in.at[i], to)

    num, den = tile(x, [far * 2, far * 2 + 1], num_own[...], den_own[...])
    num, den = num.reshape(Z, ROWS, WIDTH), den_rows(den)
    for i in range(2):
        den_copies[i].wait_recv()
        den = den + den_in[i]
        num_copies[i].wait_recv()
        num = num + num_in[i].astype(F32)
    numz_out[...] = num.astype(BF16)
    denz_out[...] = den.reshape(Z, 1, 128)
    numz, denz = Group(numz_in), Group(denz_in)
    for i, d in enumerate(z_far):
        zz = (z + d) % 8
        to = device(zz, x, y, c)
        denz.send(denz_out.at[zz], denz_in.at[i], to)
        numz.send(numz_out.at[zz], numz_in.at[i], to)
    denf.wait_recv()
    numf.wait_recv()
    num, den = num_far_out[z].astype(F32), den_far_out[z]
    for i in range(7):
        num = num + num_far_in[i].astype(F32)
        den = den + den_far_in[i]
    num_sum_out[...] = num
    den_sum_out[...] = den
    to = device(z, x_far, y, c)
    den_sum = send(den_sum_out, den_sum_in, to)
    num_sum = send(num_sum_out, num_sum_in, to)

    picks.wait_recv()
    positive = pick_in[0].astype(F32)
    for src in range(1, 8):
        positive = positive + pick_in[src].astype(F32)
    score = SHARP * jnp.sum(query.astype(F32) * positive, axis=1, keepdims=True)
    weight_p = jnp.exp(score)

    numerator = numz_out[z].astype(F32)
    den_row = denz_out[z]
    denz.wait_recv()
    numz.wait_recv()
    for i in range(7):
        den_row = den_row + denz_in[i]
        numerator = numerator + numz_in[i].astype(F32)
    den_sum.wait_recv()
    den_row = den_row + den_sum_in[...]
    num_sum.wait_recv()
    numerator = numerator + num_sum_in[...]
    denominator = jnp.sum(
        jnp.where(diagonal, jnp.broadcast_to(den_row, (ROWS, 128)), 0.0),
        axis=1,
        keepdims=True,
    )
    mass = weight_p + denominator
    grad = SHARP * ((weight_p * positive + numerator) / mass - positive)
    along = jnp.sum(grad * unit, axis=1, keepdims=True)
    grad_projected = ((grad - along * unit) / length).astype(BF16)
    gp_all[g] = grad_projected
    gps = Group(gp_all.at[pl.ds(0, 3)])
    for _, yy, cc in group_peers:
        gps.send(gp_all.at[g], gp_all.at[g], device(z, x, yy, cc))
    loss = jnp.log(mass) - score
    place = lax.broadcasted_iota(jnp.int32, (ROWS, 128), 0) + g * ROWS == (
        lax.broadcasted_iota(jnp.int32, (ROWS, 128), 1)
    )
    loss_row = jnp.sum(jnp.where(place, loss, 0.0), axis=0, keepdims=True)
    loss_rows[...] = loss_row
    losses = Group(loss_in)
    for s, yy, cc in group_peers:
        losses.send(loss_rows, loss_in.at[s - 1], device(z, x, yy, cc))
    gps.wait_recv()
    grads = jnp.dot(feat_t[...], gp_all[...].reshape(128, WIDTH), preferred_element_type=F32)
    grads = grads.reshape(Z, X, 2, 8, WIDTH)
    for xx in range(X):
        for h in range(2):
            block = grads[:, xx, h].reshape(Z * 8, WIDTH)
            wg[xx * 2 + h] = block
            wg_out[xx * 2 + h] = block.astype(BF16)
    wgx = Group(wg_in)
    for i, (dx, dy) in enumerate(rect):
        xx, yy = (x + dx) % 4, (y + dy) % 4
        wgx.send(wg_out.at[xx * 2 + yy // 2], wg_in.at[i], device(z, xx, yy, c))

    fills.wait_recv()
    first, cycle = window(g, b)
    arrived = fill_in[...].reshape(768, WIDTH)
    row = lax.broadcasted_iota(jnp.int32, (128, 128), 0)
    apart = row - lane + (first - cycle * 256)
    hit = [jnp.where(apart == 128 * m, 1.0, 0.0).astype(BF16) for m in range(3)]
    hit = jnp.concatenate(hit, axis=1)
    place_of = lax.broadcasted_iota(jnp.int32, (128, WIDTH), 0) + first
    for r in range(0, SLOT_ROWS, 128):
        moved = jnp.dot(hit, arrived[r : r + 384], preferred_element_type=F32)
        old = keys[me_col, r : r + 128, :].astype(F32)
        inside = (place_of >= -r) & (place_of < QUERIES - r)
        queue_new[r : r + 128, :] = jnp.where(inside, moved, old).astype(BF16)
    stores = [pltpu.make_async_copy(queue_new, queue_out, local_sem.at[5])]
    stores[0].start()
    losses.wait_recv()
    loss_new[...] = loss_rows[...] + loss_in[0] + loss_in[1] + loss_in[2]
    stores.append(pltpu.make_async_copy(loss_new, loss_out, local_sem.at[6]))
    stores[1].start()

    sums = wg[x * 2 + y_hi]
    wgx.wait_recv()
    for i in range(7):
        sums = sums + wg_in[i].astype(F32)
    wgz_out[...] = sums.reshape(Z, 8, WIDTH)
    wgz = Group(wgz_in)
    for i, d in enumerate(z_far):
        zz = (z + d) % 8
        wgz.send(wgz_out.at[zz], wgz_in.at[i], device(zz, x, y, c))
    total = wgz_out[z]
    wgz.wait_recv()
    for i in range(7):
        total = total + wgz_in[i]
    wgrad_new[...] = total
    stores.append(pltpu.make_async_copy(wgrad_new, wgrad_out, local_sem.at[7]))
    stores[2].start()

    assert len(groups) == COPIES
    for group in groups:
        group.wait_send()
    for copy in stores:
        copy.wait()


def local(features, weight, queue, fresh_keys, positives, write_slot):
    hbm = pl.BlockSpec(memory_space=pltpu.HBM)
    loss, weight_grad, new_queue = pl.pallas_call(
        kernel,
        out_shape=(
            jax.ShapeDtypeStruct((1, 128), F32),
            jax.ShapeDtypeStruct((8, WIDTH), F32),
            jax.ShapeDtypeStruct((SLOT_ROWS, WIDTH), BF16),
        ),
        in_specs=[hbm] * 5 + [pl.BlockSpec(memory_space=pltpu.SMEM)],
        out_specs=(hbm, hbm, hbm),
        scratch_shapes=[
            pltpu.VMEM((128, 512), BF16),
            pltpu.VMEM((512, WIDTH), BF16),
            pltpu.VMEM((4, ROWS, WIDTH), F32),
            pltpu.VMEM((3, ROWS, WIDTH), F32),
            pltpu.VMEM((X, Z, ROWS, WIDTH), BF16),
            pltpu.VMEM((8, SLOT_ROWS, WIDTH), BF16),
            pltpu.VMEM((Z, X, ROWS, WIDTH), BF16),
            pltpu.VMEM((1, 128), jnp.int32),
            pltpu.VMEM((2, 8, 128), jnp.int32),
            pltpu.VMEM((8, ROWS, WIDTH), BF16),
            pltpu.VMEM((8, ROWS, WIDTH), BF16),
            pltpu.VMEM((8, 3, ROWS, WIDTH), BF16),
            pltpu.VMEM((3, 8, ROWS, WIDTH), BF16),
            pltpu.VMEM((512, 128), BF16),
            pltpu.VMEM((Z * ROWS, WIDTH), F32),
            pltpu.VMEM((2, Z, ROWS, WIDTH), BF16),
            pltpu.VMEM((2, Z, ROWS, WIDTH), BF16),
            pltpu.VMEM((Z, ROWS, WIDTH), BF16),
            pltpu.VMEM((7, ROWS, WIDTH), BF16),
            pltpu.VMEM((ROWS, WIDTH), F32),
            pltpu.VMEM((ROWS, WIDTH), F32),
            pltpu.VMEM((Z, ROWS, WIDTH), BF16),
            pltpu.VMEM((7, ROWS, WIDTH), BF16),
            pltpu.VMEM((Z * ROWS, 128), F32),
            pltpu.VMEM((2, 8, 128), F32),
            pltpu.VMEM((2, 8, 128), F32),
            pltpu.VMEM((Z, 1, 128), F32),
            pltpu.VMEM((7, 1, 128), F32),
            pltpu.VMEM((1, 128), F32),
            pltpu.VMEM((1, 128), F32),
            pltpu.VMEM((Z, 1, 128), F32),
            pltpu.VMEM((7, 1, 128), F32),
            pltpu.VMEM((4, ROWS, WIDTH), BF16),
            pltpu.VMEM((1, 128), F32),
            pltpu.VMEM((3, 1, 128), F32),
            pltpu.VMEM((8, Z * 8, WIDTH), F32),
            pltpu.VMEM((8, Z * 8, WIDTH), BF16),
            pltpu.VMEM((7, Z * 8, WIDTH), BF16),
            pltpu.VMEM((Z, 8, WIDTH), F32),
            pltpu.VMEM((7, 8, WIDTH), F32),
            pltpu.VMEM((SLOT_ROWS, WIDTH), BF16),
            pltpu.VMEM((1, 128), F32),
            pltpu.VMEM((8, WIDTH), F32),
            pltpu.SemaphoreType.DMA((8,)),
            pltpu.SemaphoreType.DMA((COPIES,)),
            pltpu.SemaphoreType.DMA((COPIES,)),
        ],
        compiler_params=pltpu.CompilerParams(
            collective_id=0, has_side_effects=True, vmem_limit_bytes=60 << 20
        ),
        name="retrieval_step",
    )(features, weight, queue, fresh_keys, positives.reshape(1, 128), write_slot)
    return loss.reshape(128), weight_grad, new_queue


def solution(mesh):
    in_specs = (
        P("blk", "group"),
        P("group", None),
        P(("group", "blk"), None),
        P("blk", None),
        P("blk"),
        P(),
    )
    out_specs = (P("blk"), P(("group", "blk"), None), P(("group", "blk"), None))
    return jax.shard_map(local, mesh=mesh, in_specs=in_specs, out_specs=out_specs, check_vma=False)
```

time: 68.7 us -> 58.2 us (0.85)
  Pallas kernels: 60.8 us -> 53.3 us
  local copies, waits for them, and re-layouts: 6.1 us -> 3.46 us
    pallas_call x1, Pallas kernels: 60.8 us -> 53.3 us  [local(): pl.pallas_call(kernel, out_shape=(jax.ShapeDtypeStruct((1, 128), F32), ja...]
    unnamed x13 -> x5, local copies, waits for them, and re-layouts: 6.1 us -> 3.46 us
where the time goes in v3:
time: 58.2 us; the launch traced here: 58 us
  Pallas kernels  53.3 us (92%)
  local copies, waits for them, and re-layouts  3.46 us (6%)
  between operations  1.3 us (2%)
    pallas_call x1, Pallas kernels, local(): pl.pallas_call(kernel, out_shape=(jax.ShapeDtypeStruct((1, 128), F32), ja...  53.3 us
    unnamed x5, local copies, waits for them, and re-layouts  3.46 us

profile of v3, /device:TPU:1, one launch (start us, length us, event | category | flops | bytes accessed | tf_op | source)
XLA Modules:
  0.0 58.0 jit_solution(1261107237126738170)
XLA Ops:
  1.3 53.3 %retrieval_step.1 = (f32[1,128]{1,0:T(1,128)}, f32[8,256]{1,0:T(8,128)}, bf16[512,256]{1,0:T(8,128)(2,1)}) custom-call(bf16[128,512]{1,0:T(8,128)(2,1)} %features_hbm.1, bf16[512,256]{1,0:T(8,128)(2,1)} %weight_hbm.1, bf16[512,256]{1,0:T(8,128)(2,1)} %queue_hbm.1, bf16[128,256]{1,0:T(8,128)(2,1)} %fresh_hbm.1, s32[1,128]{1,0:T(1,128)} %bitcast.2, ...), custom_call_target="tpu_custom_call" | custom-call | tf_op jit(solution)/shard_map/retrieval_step/pallas_call | solution.py:463
  54.6 0.0 copy-start
  54.6 1.2 %copy.13 = f32[128]{0:T(128)} copy(f32[128]{0:T(128)} %bitcast.3) | data formatting | bytes 1024
  55.8 0.0 copy-done
  55.8 0.6 %copy.14 = f32[8,256]{1,0:T(8,128)} copy(f32[8,256]{1,0:T(8,128)S(1)} %copy-done) | data formatting | bytes 16384
  56.4 1.7 %copy.15 = bf16[512,256]{1,0:T(8,128)(2,1)} copy(bf16[512,256]{1,0:T(8,128)(2,1)} %get-tuple-element.14) | data formatting | bytes 524288
Async XLA Ops:
  54.6 1.2 %copy-start = (f32[8,256]{1,0:T(8,128)S(1)}, f32[8,256]{1,0:T(8,128)}, u32[]{:S(2)}) copy-start(f32[8,256]{1,0:T(8,128)} %get-tuple-element.13) | copy-start | bytes 24580

commit v4 on v3

--- a/solution.py
+++ b/solution.py
@@ -19,7 +19,8 @@
 QUERIES = 8192
 F32 = jnp.float32
 BF16 = jnp.bfloat16
-COPIES = 47
+COPIES = 41
+LARGE, SMALL = 1043, 34
 
 
 def lane_sums(e):
@@ -53,6 +54,7 @@
     fill_out,
     fill_in,
     feat_t,
+    feat_z,
     num_own,
     num_out,
     num_in,
@@ -69,19 +71,26 @@
     den_far_in,
     den_sum_out,
     den_sum_in,
+    den_line,
     denz_out,
     denz_in,
     gp_all,
     loss_rows,
     loss_in,
     wg,
-    wg_out,
-    wg_in,
+    wgx_out,
+    wgx_in,
     wgz_out,
     wgz_in,
+    wgx2_out,
+    wgx2_in,
+    wgz2_out,
+    wgz2_in,
     queue_new,
     loss_new,
     wgrad_new,
+    sent_large,
+    sent_small,
     local_sem,
     send_sem,
     recv_sem,
@@ -111,7 +120,10 @@
     def device(zz, xx, yy, cc):
         return {"group": (yy % 2) * 2 + cc, "blk": zz * 8 + xx * 2 + yy // 2}
 
-    groups = []
+    groups, sent = [], [0, 0]
+
+    def small(ref):
+        return int(ref.shape[-2] == 1)
 
     class Group:
         def __init__(self, whole):
@@ -122,21 +134,19 @@
             return pltpu.make_async_remote_copy(
                 src_ref=src,
                 dst_ref=dst,
-                send_sem=send_sem.at[self.at],
+                send_sem=send_sem.at[small(src)],
                 recv_sem=recv_sem.at[self.at],
                 device_id=to,
                 device_id_type=pl.DeviceIdType.MESH,
             )
 
         def send(self, src, dst, to):
+            sent[small(src)] += math.prod(src.shape) * src.dtype.itemsize
             self.copy(src, dst, to).start()
 
         def wait_recv(self):
             self.got = True
             self.copy(self.whole, self.whole, neighbour).wait_recv()
-
-        def wait_send(self):
-            self.copy(self.whole, self.whole, neighbour).wait_send()
 
     neighbour = device(z, x, y, 1 - c)
 
@@ -148,6 +158,7 @@
     column = [(dy, dc) for dy in (0, 1, 3, 2) for dc in (1, 0) if (dy, dc) != (0, 0)]
     z_order = (1, 7, 2, 6, 3, 5, 4)
     z_far = (4, 3, 5, 2, 6, 1, 7)
+    z_line = (0, *z_order)
     rect = [(dx, dy) for dx in (2, 1, 3, 0) for dy in (2, 0) if (dx, dy) != (0, 0)]
     x_near, x_far = (x + 1) % 4, (x + 2) % 4
     x_back = (x + 3) % 4
@@ -196,7 +207,9 @@
 
     up_low = pass_on(y, 0, to_up)
     down_high = pass_on(y, 1, to_down)
-    key_other = [pass_on(y, h, to_other) for h in range(2)]
+    key_other = Group(keys.at[pl.ds(0, 3)])
+    for h in range(2):
+        key_other.send(part(y, h), part(y, h), to_other)
     up_high = pass_on(y, 1, to_up)
     down_low = pass_on(y, 0, to_down)
     pos_copy = send(pos_all.at[0], pos_all.at[1], device(z, x, far, c))
@@ -208,11 +221,11 @@
     query = unit.astype(BF16)
     queries[x, z] = query
     own_q = queries.at[x, z]
-    qx = {d: Group(queries.at[x]) for d in (1, 3)}
+    qx = [Group(queries.at[pl.ds(0, 2), pl.ds(0, 4)]) for _ in range(2)]
     query_far = send(own_q, own_q, device(z, x_far, y, c))
     qz = {d: send(own_q, own_q, device((z + d) % 8, x, y, c)) for d in z_order}
     for d in (1, 3):
-        qx[d].send(own_q, own_q, device(z, (x + d) % 4, y, c))
+        qx[0].send(own_q, own_q, device(z, (x + d) % 4, y, c))
     fresh_far.wait_recv()
     block = fresh_all.at[z, x_far]
     fz_far = Group(fresh_all.at[pl.ds(0, 7), x])
@@ -223,14 +236,19 @@
     fx = Group(fresh_all.at[:, pl.ds(0, 2)])
     for xx in (x_near, x_back):
         fx.send(fresh_line, fresh_line, device(z, xx, y, c))
-    feat_t[...] = features[...].T
+    turned = features[...].astype(F32).T
+    feat_z[...] = turned.astype(BF16).reshape(8, 64, 128)
+    turned = turned.reshape(Z, X, 2, 8, 128)
+    for xx in range(X):
+        for h in range(2):
+            feat_t[xx * 2 + h] = turned[:, xx, h].reshape(Z * 8, 128).astype(BF16)
 
     up_low.wait_recv()
     far_low = pass_on(down, 0, to_up)
-    key_other.append(pass_on(down, 0, to_other))
+    key_other.send(part(down, 0), part(down, 0), to_other)
     down_high.wait_recv()
     far_high = pass_on(up, 1, to_down)
-    key_other.append(pass_on(up, 1, to_other))
+    key_other.send(part(up, 1), part(up, 1), to_other)
     query_far.wait_recv()
     block = queries.at[x_far, z]
     qz_far = Group(queries.at[x, pl.ds(0, 7)])
@@ -240,20 +258,19 @@
         qz[d].wait_recv()
         block = queries.at[x, (z + 8 - d) % 8]
         for e in (1, 3):
-            qx[e].send(block, block, device(z, (x + e) % 4, y, c))
+            qx[z_line.index(d) // 4].send(block, block, device(z, (x + e) % 4, y, c))
     up_high.wait_recv()
-    key_other.append(pass_on(down, 1, to_other))
+    key_other.send(part(down, 1), part(down, 1), to_other)
     down_low.wait_recv()
-    key_other.append(pass_on(up, 0, to_other))
-    for copy in key_other:
-        copy.wait_recv()
+    key_other.send(part(up, 0), part(up, 0), to_other)
+    key_other.wait_recv()
 
     diagonal = lax.broadcasted_iota(jnp.int32, (ROWS, 128), 0) == lax.broadcasted_iota(
         jnp.int32, (ROWS, 128), 1
     )
 
-    def tile(xx, where, num=None, den=None):
-        q = queries[xx].reshape(Z * ROWS, WIDTH)
+    def tile(q, where, num=None, den=None):
+        q = q.reshape(Z * ROWS, WIDTH)
         for j in where:
             k = keys[j]
             s = lax.dot_general(q, k, (((1,), (1,)), ((), ())), preferred_element_type=F32)
@@ -266,13 +283,14 @@
 
     def den_rows(den):
         column_sums = jnp.sum(den, axis=1, keepdims=True).reshape(Z, ROWS, 1)
-        return jnp.sum(jnp.where(diagonal[None], column_sums, 0.0), axis=1)
-
-    num_own[...], den_own[...] = tile(x, [yy * 2 + cc for yy in (y, down, up) for cc in (0, 1)])
+        return jnp.sum(jnp.where(diagonal[None], column_sums, 0.0), axis=1).reshape(Z, 1, 128)
+
+    num_own[...], den_own[...] = tile(queries[x], [yy * 2 + cc for yy in (y, down, up) for cc in (0, 1)])
     far_low.wait_recv()
-    far_other = [pass_on(far, 0, to_other)]
+    far_other = Group(keys.at[0])
+    far_other.send(part(far, 0), part(far, 0), to_other)
     far_high.wait_recv()
-    far_other.append(pass_on(far, 1, to_other))
+    far_other.send(part(far, 1), part(far, 1), to_other)
 
     fz_far.wait_recv()
     fx.wait_recv()
@@ -311,44 +329,54 @@
         fills.send(fill_out.at[yy * 2 + cc], fill_in.at[:, me_col], to)
     fill_in[:, me_col] = fill_out[me_col]
 
-    for copy in far_other:
-        copy.wait_recv()
-    num_copies, den_copies = [], []
-    for i, d in enumerate((1, 3)):
-        qx[d].wait_recv()
-        owner = (x + 4 - d) % 4
-        num, den = tile(owner, range(8))
-        num_out[i] = num.astype(BF16).reshape(Z, ROWS, WIDTH)
-        den_out[i] = den_rows(den)
-        to = device(z, owner, y, c)
-        den_copies.append(send(den_out.at[i], den_in.at[i], to))
-        num_copies.append(send(num_out.at[i], num_in.at[i], to))
+    far_other.wait_recv()
+    num_near, den_near = Group(num_in), Group(den_in)
+
+    def near_tile(h):
+        qx[h].wait_recv()
+        rows = pl.ds(4 * h, 4)
+        line = [(z + 8 - d) % 8 for d in z_line[4 * h : 4 * h + 4]]
+        q = jnp.concatenate([queries[xx, zz] for xx in (x_back, x_near) for zz in line], axis=0)
+        num, den = tile(q, range(8))
+        num, den = num.astype(BF16).reshape(Z, ROWS, WIDTH), den_rows(den)
+        for i, owner in enumerate((x_back, x_near)):
+            to = device(z, owner, y, c)
+            num_out[i, rows] = num[4 * i : 4 * i + 4]
+            den_out[i, rows] = den[4 * i : 4 * i + 4]
+            num_near.send(num_out.at[i, rows], num_in.at[i, rows], to)
+            den_near.send(den_out.at[i, rows], den_in.at[i, rows], to)
+
+    near_tile(0)
     qz_far.wait_recv()
-    num, den = tile(x_far, range(8))
+    num, den = tile(queries[x_far], range(8))
     num_far_out[...] = num.astype(BF16).reshape(Z, ROWS, WIDTH)
-    den_far_out[...] = den_rows(den).reshape(Z, 1, 128)
+    den_far_out[...] = den_rows(den)
     numf, denf = Group(num_far_in), Group(den_far_in)
     for i, d in enumerate(z_far):
         zz = (z + d) % 8
         to = device(zz, x, y, c)
         denf.send(den_far_out.at[zz], den_far_in.at[i], to)
         numf.send(num_far_out.at[zz], num_far_in.at[i], to)
-
-    num, den = tile(x, [far * 2, far * 2 + 1], num_own[...], den_own[...])
-    num, den = num.reshape(Z, ROWS, WIDTH), den_rows(den)
-    for i in range(2):
-        den_copies[i].wait_recv()
-        den = den + den_in[i]
-        num_copies[i].wait_recv()
-        num = num + num_in[i].astype(F32)
-    numz_out[...] = num.astype(BF16)
-    denz_out[...] = den.reshape(Z, 1, 128)
+    near_tile(1)
+
+    num_own[...], den = tile(queries[x], [far * 2, far * 2 + 1], num_own[...], den_own[...])
+    den_line[...] = den_rows(den)
     numz, denz = Group(numz_in), Group(denz_in)
+    den_near.wait_recv()
+    num_near.wait_recv()
+
+    def own_block(d):
+        zz, at = (z + d) % 8, z_line.index((8 - d) % 8)
+        rows = pl.ds(pl.multiple_of(zz * ROWS, ROWS), ROWS)
+        num = num_own[rows] + num_in[0, at].astype(F32) + num_in[1, at].astype(F32)
+        return num, den_line[zz] + den_in[0, at] + den_in[1, at]
+
     for i, d in enumerate(z_far):
-        zz = (z + d) % 8
-        to = device(zz, x, y, c)
-        denz.send(denz_out.at[zz], denz_in.at[i], to)
-        numz.send(numz_out.at[zz], numz_in.at[i], to)
+        to = device((z + d) % 8, x, y, c)
+        num, den = own_block(d)
+        numz_out[i], denz_out[i] = num.astype(BF16), den
+        numz.send(numz_out.at[i], numz_in.at[i], to)
+        denz.send(denz_out.at[i], denz_in.at[i], to)
     denf.wait_recv()
     numf.wait_recv()
     num, den = num_far_out[z].astype(F32), den_far_out[z]
@@ -368,8 +396,7 @@
     score = SHARP * jnp.sum(query.astype(F32) * positive, axis=1, keepdims=True)
     weight_p = jnp.exp(score)
 
-    numerator = numz_out[z].astype(F32)
-    den_row = denz_out[z]
+    numerator, den_row = own_block(0)
     denz.wait_recv()
     numz.wait_recv()
     for i in range(7):
@@ -402,17 +429,20 @@
     for s, yy, cc in group_peers:
         losses.send(loss_rows, loss_in.at[s - 1], device(z, x, yy, cc))
     gps.wait_recv()
-    grads = jnp.dot(feat_t[...], gp_all[...].reshape(128, WIDTH), preferred_element_type=F32)
-    grads = grads.reshape(Z, X, 2, 8, WIDTH)
-    for xx in range(X):
-        for h in range(2):
-            block = grads[:, xx, h].reshape(Z * 8, WIDTH)
-            wg[xx * 2 + h] = block
-            wg_out[xx * 2 + h] = block.astype(BF16)
-    wgx = Group(wg_in)
+    grads = gp_all[...].reshape(128, WIDTH)
+    left, right = grads[:, :128], grads[:, 128:]
+    wgx, wgz = Group(wgx_in), Group(wgz_in)
     for i, (dx, dy) in enumerate(rect):
         xx, yy = (x + dx) % 4, (y + dy) % 4
-        wgx.send(wg_out.at[xx * 2 + yy // 2], wg_in.at[i], device(z, xx, yy, c))
+        at = xx * 2 + yy // 2
+        wgx_out[i] = jnp.dot(feat_t[at], left, preferred_element_type=F32).astype(BF16)
+        wgx.send(wgx_out.at[i], wgx_in.at[i], device(z, xx, yy, c))
+        zz = (z + z_far[i]) % 8
+        wgz_out[i] = jnp.dot(feat_z[zz], right, preferred_element_type=F32).astype(BF16)
+        wgz.send(wgz_out.at[i], wgz_in.at[i], device(zz, x, y, c))
+    me_rect = x * 2 + y_hi
+    wg[0] = jnp.dot(feat_t[me_rect], left, preferred_element_type=F32)
+    wg[1] = jnp.dot(feat_z[z], right, preferred_element_type=F32)
 
     fills.wait_recv()
     first, cycle = window(g, b)
@@ -434,26 +464,47 @@
     stores.append(pltpu.make_async_copy(loss_new, loss_out, local_sem.at[6]))
     stores[1].start()
 
-    sums = wg[x * 2 + y_hi]
+    sums = wg[1]
+    wgz.wait_recv()
+    for i in range(7):
+        sums = sums + wgz_in[i].astype(F32)
+    wgx2_out[...] = sums.reshape(8, 8, 128)
+    wgx2, wgz2 = Group(wgx2_in), Group(wgz2_in)
+    for i, (dx, dy) in enumerate(rect):
+        xx, yy = (x + dx) % 4, (y + dy) % 4
+        wgx2.send(wgx2_out.at[xx * 2 + yy // 2], wgx2_in.at[i], device(z, xx, yy, c))
+    sums = wg[0]
     wgx.wait_recv()
     for i in range(7):
-        sums = sums + wg_in[i].astype(F32)
-    wgz_out[...] = sums.reshape(Z, 8, WIDTH)
-    wgz = Group(wgz_in)
+        sums = sums + wgx_in[i].astype(F32)
+    wgz2_out[...] = sums.reshape(Z, 8, 128)
     for i, d in enumerate(z_far):
         zz = (z + d) % 8
-        wgz.send(wgz_out.at[zz], wgz_in.at[i], device(zz, x, y, c))
-    total = wgz_out[z]
-    wgz.wait_recv()
+        wgz2.send(wgz2_out.at[zz], wgz2_in.at[i], device(zz, x, y, c))
+    total = wgx2_out[me_rect]
+    wgx2.wait_recv()
     for i in range(7):
-        total = total + wgz_in[i]
-    wgrad_new[...] = total
+        total = total + wgx2_in[i]
+    wgrad_new[:, 128:] = total
+    total = wgz2_out[z]
+    wgz2.wait_recv()
+    for i in range(7):
+        total = total + wgz2_in[i]
+    wgrad_new[:, :128] = total
     stores.append(pltpu.make_async_copy(wgrad_new, wgrad_out, local_sem.at[7]))
     stores[2].start()
 
     assert len(groups) == COPIES
-    for group in groups:
-        group.wait_send()
+    for i, all_sent in enumerate((sent_large, sent_small)):
+        assert sent[i] == math.prod(all_sent.shape) * 4, sent
+        pltpu.make_async_remote_copy(
+            src_ref=all_sent,
+            dst_ref=all_sent,
+            send_sem=send_sem.at[i],
+            recv_sem=recv_sem.at[0],
+            device_id=neighbour,
+            device_id_type=pl.DeviceIdType.MESH,
+        ).wait_send()
     for copy in stores:
         copy.wait()
 
@@ -483,7 +534,8 @@
             pltpu.VMEM((8, ROWS, WIDTH), BF16),
             pltpu.VMEM((8, 3, ROWS, WIDTH), BF16),
             pltpu.VMEM((3, 8, ROWS, WIDTH), BF16),
-            pltpu.VMEM((512, 128), BF16),
+            pltpu.VMEM((8, Z * 8, 128), BF16),
+            pltpu.VMEM((8, 64, 128), BF16),
             pltpu.VMEM((Z * ROWS, WIDTH), F32),
             pltpu.VMEM((2, Z, ROWS, WIDTH), BF16),
             pltpu.VMEM((2, Z, ROWS, WIDTH), BF16),
@@ -491,30 +543,37 @@
             pltpu.VMEM((7, ROWS, WIDTH), BF16),
             pltpu.VMEM((ROWS, WIDTH), F32),
             pltpu.VMEM((ROWS, WIDTH), F32),
-            pltpu.VMEM((Z, ROWS, WIDTH), BF16),
+            pltpu.VMEM((7, ROWS, WIDTH), BF16),
             pltpu.VMEM((7, ROWS, WIDTH), BF16),
             pltpu.VMEM((Z * ROWS, 128), F32),
-            pltpu.VMEM((2, 8, 128), F32),
-            pltpu.VMEM((2, 8, 128), F32),
+            pltpu.VMEM((2, Z, 1, 128), F32),
+            pltpu.VMEM((2, Z, 1, 128), F32),
             pltpu.VMEM((Z, 1, 128), F32),
             pltpu.VMEM((7, 1, 128), F32),
             pltpu.VMEM((1, 128), F32),
             pltpu.VMEM((1, 128), F32),
             pltpu.VMEM((Z, 1, 128), F32),
             pltpu.VMEM((7, 1, 128), F32),
+            pltpu.VMEM((7, 1, 128), F32),
             pltpu.VMEM((4, ROWS, WIDTH), BF16),
             pltpu.VMEM((1, 128), F32),
             pltpu.VMEM((3, 1, 128), F32),
-            pltpu.VMEM((8, Z * 8, WIDTH), F32),
-            pltpu.VMEM((8, Z * 8, WIDTH), BF16),
-            pltpu.VMEM((7, Z * 8, WIDTH), BF16),
-            pltpu.VMEM((Z, 8, WIDTH), F32),
-            pltpu.VMEM((7, 8, WIDTH), F32),
+            pltpu.VMEM((2, 64, 128), F32),
+            pltpu.VMEM((7, 64, 128), BF16),
+            pltpu.VMEM((7, 64, 128), BF16),
+            pltpu.VMEM((7, 64, 128), BF16),
+            pltpu.VMEM((7, 64, 128), BF16),
+            pltpu.VMEM((8, 8, 128), F32),
+            pltpu.VMEM((7, 8, 128), F32),
+            pltpu.VMEM((8, 8, 128), F32),
+            pltpu.VMEM((7, 8, 128), F32),
             pltpu.VMEM((SLOT_ROWS, WIDTH), BF16),
             pltpu.VMEM((1, 128), F32),
             pltpu.VMEM((8, WIDTH), F32),
+            pltpu.VMEM((LARGE, 8, 128), F32),
+            pltpu.VMEM((SMALL, 1, 128), F32),
             pltpu.SemaphoreType.DMA((8,)),
-            pltpu.SemaphoreType.DMA((COPIES,)),
+            pltpu.SemaphoreType.DMA((2,)),
             pltpu.SemaphoreType.DMA((COPIES,)),
         ],
         compiler_params=pltpu.CompilerParams(

time: 58.2 us -> 57.5 us (0.988)
  Pallas kernels: 53.3 us -> 52.5 us
    pallas_call x1, Pallas kernels: 53.3 us -> 52.5 us  [local(): pl.pallas_call(kernel, out_shape=(jax.ShapeDtypeStruct((1, 128), F32), ja...]
where the time goes in v4:
time: 57.5 us; the launch traced here: 57.3 us
  Pallas kernels  52.5 us (91%)
  local copies, waits for them, and re-layouts  3.46 us (6%)
  between operations  1.3 us (2%)
    pallas_call x1, Pallas kernels, local(): pl.pallas_call(kernel, out_shape=(jax.ShapeDtypeStruct((1, 128), F32), ja...  52.5 us
    unnamed x5, local copies, waits for them, and re-layouts  3.46 us

profile of v4, /device:TPU:1, one launch (start us, length us, event | category | flops | bytes accessed | tf_op | source)
XLA Modules:
  0.0 57.3 jit_solution(4882346410957252875)
XLA Ops:
  1.3 52.5 %retrieval_step.1 = (f32[1,128]{1,0:T(1,128)}, f32[8,256]{1,0:T(8,128)}, bf16[512,256]{1,0:T(8,128)(2,1)}) custom-call(bf16[128,512]{1,0:T(8,128)(2,1)} %features_hbm.1, bf16[512,256]{1,0:T(8,128)(2,1)} %weight_hbm.1, bf16[512,256]{1,0:T(8,128)(2,1)} %queue_hbm.1, bf16[128,256]{1,0:T(8,128)(2,1)} %fresh_hbm.1, s32[1,128]{1,0:T(1,128)} %bitcast.2, ...), custom_call_target="tpu_custom_call" | custom-call | tf_op jit(solution)/shard_map/retrieval_step/pallas_call | solution.py:514
  53.8 0.0 copy-start
  53.8 1.2 %copy.13 = f32[128]{0:T(128)} copy(f32[128]{0:T(128)} %bitcast.3) | data formatting | bytes 1024
  55.0 0.0 copy-done
  55.0 0.6 %copy.14 = f32[8,256]{1,0:T(8,128)} copy(f32[8,256]{1,0:T(8,128)S(1)} %copy-done) | data formatting | bytes 16384
  55.6 1.7 %copy.15 = bf16[512,256]{1,0:T(8,128)(2,1)} copy(bf16[512,256]{1,0:T(8,128)(2,1)} %get-tuple-element.14) | data formatting | bytes 524288
Async XLA Ops:
  53.8 1.2 %copy-start = (f32[8,256]{1,0:T(8,128)S(1)}, f32[8,256]{1,0:T(8,128)}, u32[]{:S(2)}) copy-start(f32[8,256]{1,0:T(8,128)} %get-tuple-element.13) | copy-start | bytes 24580

commit v5 on v4

--- a/solution.py
+++ b/solution.py
@@ -292,6 +292,39 @@
     far_high.wait_recv()
     far_other.send(part(far, 1), part(far, 1), to_other)
 
+    far_other.wait_recv()
+    num_near, den_near = Group(num_in), Group(den_in)
+
+    def near_tile(h):
+        qx[h].wait_recv()
+        rows = pl.ds(4 * h, 4)
+        line = [(z + 8 - d) % 8 for d in z_line[4 * h : 4 * h + 4]]
+        q = jnp.concatenate([queries[xx, zz] for xx in (x_back, x_near) for zz in line], axis=0)
+        num, den = tile(q, range(8))
+        num, den = num.astype(BF16).reshape(Z, ROWS, WIDTH), den_rows(den)
+        for i, owner in enumerate((x_back, x_near)):
+            to = device(z, owner, y, c)
+            num_out[i, rows] = num[4 * i : 4 * i + 4]
+            den_out[i, rows] = den[4 * i : 4 * i + 4]
+            num_near.send(num_out.at[i, rows], num_in.at[i, rows], to)
+            den_near.send(den_out.at[i, rows], den_in.at[i, rows], to)
+
+    near_tile(0)
+    qz_far.wait_recv()
+    num, den = tile(queries[x_far], range(8))
+    num_far_out[...] = num.astype(BF16).reshape(Z, ROWS, WIDTH)
+    den_far_out[...] = den_rows(den)
+    numf, denf = Group(num_far_in), Group(den_far_in)
+    for i, d in enumerate(z_far):
+        zz = (z + d) % 8
+        to = device(zz, x, y, c)
+        denf.send(den_far_out.at[zz], den_far_in.at[i], to)
+        numf.send(num_far_out.at[zz], num_far_in.at[i], to)
+    near_tile(1)
+
+    num_own[...], den = tile(queries[x], [far * 2, far * 2 + 1], num_own[...], den_own[...])
+    den_line[...] = den_rows(den)
+    numz, denz = Group(numz_in), Group(denz_in)
     fz_far.wait_recv()
     fx.wait_recv()
     pos_copy.wait_recv()
@@ -329,39 +362,6 @@
         fills.send(fill_out.at[yy * 2 + cc], fill_in.at[:, me_col], to)
     fill_in[:, me_col] = fill_out[me_col]
 
-    far_other.wait_recv()
-    num_near, den_near = Group(num_in), Group(den_in)
-
-    def near_tile(h):
-        qx[h].wait_recv()
-        rows = pl.ds(4 * h, 4)
-        line = [(z + 8 - d) % 8 for d in z_line[4 * h : 4 * h + 4]]
-        q = jnp.concatenate([queries[xx, zz] for xx in (x_back, x_near) for zz in line], axis=0)
-        num, den = tile(q, range(8))
-        num, den = num.astype(BF16).reshape(Z, ROWS, WIDTH), den_rows(den)
-        for i, owner in enumerate((x_back, x_near)):
-            to = device(z, owner, y, c)
-            num_out[i, rows] = num[4 * i : 4 * i + 4]
-            den_out[i, rows] = den[4 * i : 4 * i + 4]
-            num_near.send(num_out.at[i, rows], num_in.at[i, rows], to)
-            den_near.send(den_out.at[i, rows], den_in.at[i, rows], to)
-
-    near_tile(0)
-    qz_far.wait_recv()
-    num, den = tile(queries[x_far], range(8))
-    num_far_out[...] = num.astype(BF16).reshape(Z, ROWS, WIDTH)
-    den_far_out[...] = den_rows(den)
-    numf, denf = Group(num_far_in), Group(den_far_in)
-    for i, d in enumerate(z_far):
-        zz = (z + d) % 8
-        to = device(zz, x, y, c)
-        denf.send(den_far_out.at[zz], den_far_in.at[i], to)
-        numf.send(num_far_out.at[zz], num_far_in.at[i], to)
-    near_tile(1)
-
-    num_own[...], den = tile(queries[x], [far * 2, far * 2 + 1], num_own[...], den_own[...])
-    den_line[...] = den_rows(den)
-    numz, denz = Group(numz_in), Group(denz_in)
     den_near.wait_recv()
     num_near.wait_recv()
 

time: 57.5 us -> 57.3 us (level)
  no operation moved by 1% of the time
where the time goes in v5:
time: 57.3 us; the launch traced here: 57.1 us
  Pallas kernels  52.4 us (91%)
  local copies, waits for them, and re-layouts  3.46 us (6%)
  between operations  1.3 us (2%)
    pallas_call x1, Pallas kernels, local(): pl.pallas_call(kernel, out_shape=(jax.ShapeDtypeStruct((1, 128), F32), ja...  52.4 us
    unnamed x5, local copies, waits for them, and re-layouts  3.46 us

profile of v5, /device:TPU:1, one launch (start us, length us, event | category | flops | bytes accessed | tf_op | source)
XLA Modules:
  0.0 57.1 jit_solution(14246033916627224517)
XLA Ops:
  1.3 52.4 %retrieval_step.1 = (f32[1,128]{1,0:T(1,128)}, f32[8,256]{1,0:T(8,128)}, bf16[512,256]{1,0:T(8,128)(2,1)}) custom-call(bf16[128,512]{1,0:T(8,128)(2,1)} %features_hbm.1, bf16[512,256]{1,0:T(8,128)(2,1)} %weight_hbm.1, bf16[512,256]{1,0:T(8,128)(2,1)} %queue_hbm.1, bf16[128,256]{1,0:T(8,128)(2,1)} %fresh_hbm.1, s32[1,128]{1,0:T(1,128)} %bitcast.2, ...), custom_call_target="tpu_custom_call" | custom-call | tf_op jit(solution)/shard_map/retrieval_step/pallas_call | solution.py:514
  53.7 0.0 copy-start
  53.7 1.2 %copy.13 = f32[128]{0:T(128)} copy(f32[128]{0:T(128)} %bitcast.3) | data formatting | bytes 1024
  54.9 0.0 copy-done
  54.9 0.6 %copy.14 = f32[8,256]{1,0:T(8,128)} copy(f32[8,256]{1,0:T(8,128)S(1)} %copy-done) | data formatting | bytes 16384
  55.5 1.7 %copy.15 = bf16[512,256]{1,0:T(8,128)(2,1)} copy(bf16[512,256]{1,0:T(8,128)(2,1)} %get-tuple-element.14) | data formatting | bytes 524288
Async XLA Ops:
  53.7 1.2 %copy-start = (f32[8,256]{1,0:T(8,128)S(1)}, f32[8,256]{1,0:T(8,128)}, u32[]{:S(2)}) copy-start(f32[8,256]{1,0:T(8,128)} %get-tuple-element.13) | copy-start | bytes 24580
